TPU v7x, 512 devices: a whole 4x8x8 slice. The times are simulated.
512 devices in a mesh: lon: 128 (over x_lo, z, y), lat: 4 (over x_hi, core).
Axes of the slice: x: 4 (x_hi: 2, x_lo: 2; x = x_hi * 2 + x_lo), y: 8, z: 8, core: 2. Of those that a mesh axis runs over, the one named last changes fastest.
Arguments:
- features: bfloat16 [320, 2048, 384], P('lat', 'lon'), may hold values from -6 to 6
- filter_basis: bfloat16 [3, 5, 17, 320], replicated, may hold values from -0.8984375 to 0.8984375
- half_widths: int32 [320], replicated, may hold values from 1 to 8, as said below
- mixing: bfloat16 [1152, 384], replicated, may hold values from -0.1875 to 0.1875
- channel_bias: float32 [384], replicated, may hold values from -3 to 3
- cotangent: bfloat16 [320, 2048, 384], P('lat', 'lon'), may hold values from -6 to 6
Outputs:
- input_grad: bfloat16 [320, 2048, 384], P('lat', 'lon')
- mixing_grad: bfloat16 [1152, 384], replicated
Inputs may be any that keep to these rules, and one draw needn't show every extreme that they name: `half_widths`: the first and last latitude rows have exactly 8.
All inputs are finite; a program needn't handle non-finite values.
Results may differ from a plain program's by a relative error of at most 0.0063.
Values may be sent and summed in bfloat16 or wider, within the bound.
A program may use at most 128 MiB of HBM per device.

v0:
```python
import math

import jax
import jax.numpy as jnp
from jax import lax
from jax.sharding import PartitionSpec as P


def extended_2(block, sides, width, periodic):
    for axis, dim in sides:
        count = lax.axis_size(axis)
        forward = [(i, i + 1) for i in range(count - 1)]
        if periodic:
            forward.append((count - 1, 0))
        backward = [(target, source) for source, target in forward]
        low = lax.ppermute(
            lax.slice_in_dim(block, block.shape[dim] - width, None, axis=dim), axis, forward
        )
        high = lax.ppermute(lax.slice_in_dim(block, 0, width, axis=dim), axis, backward)
        block = jnp.concatenate([low, block, high], axis=dim)
    return block


def gelu_exact(values):
    return jax.nn.gelu(values, approximate=False)


def basis_window(filter_basis, half_widths, row_start, rows_here, reach, halo):
    taps_lon = 2 * halo + 1
    offsets = jnp.abs(jnp.arange(taps_lon, dtype=jnp.int32) - halo)
    allowed = (offsets[:, None] <= half_widths[None, :]).astype(jnp.float32)
    masked = filter_basis.astype(jnp.float32) * allowed[None, None]
    padded = jnp.pad(masked, ((0, 0), (0, 0), (0, 0), (reach, reach)))
    return lax.dynamic_slice_in_dim(padded, row_start, rows_here + 2 * reach, 3)


def band_matrix(rows_taps, shift_table):
    band = jnp.einsum("bsqa,qvu->avbsu", rows_taps, shift_table, precision=lax.Precision.HIGHEST)
    count_rows, width_out, kernels, taps_lat, width_in = band.shape
    return band.reshape(count_rows, width_out * kernels, taps_lat * width_in).astype(jnp.bfloat16)


def stacked_rows(extended, rows_here, taps_lat):
    pieces = [extended[offset : offset + rows_here] for offset in range(taps_lat)]
    stacked = jnp.stack(pieces, axis=1)
    return stacked.reshape(rows_here, -1, stacked.shape[-1])


def contract(band, windows):
    return jnp.einsum("anm,amc->anc", band, windows, preferred_element_type=jnp.float32)


def extend_lat(block, reach):
    return extended_2(block, (("lat", 0),), reach, False)


def apply_band(band, lat_ext, halo, rows_here, taps_lat):
    padded = extended_2(lat_ext, (("lon", 1),), halo, True)
    return contract(band, stacked_rows(padded, rows_here, taps_lat))


def per_device(features, filter_basis, half_widths, mixing, channel_bias, cotangent):
    rows_here, width_here, channels = features.shape
    kernels, taps_lat, taps_lon, total_rows = filter_basis.shape
    reach = (taps_lat - 1) // 2
    halo = (taps_lon - 1) // 2
    row_start = lax.axis_index("lat") * rows_here
    window = basis_window(filter_basis, half_widths, row_start, rows_here, reach, halo)
    span = width_here + 2 * halo
    tap_ids = jnp.arange(taps_lon, dtype=jnp.int32)[:, None, None]
    out_ids = jnp.arange(width_here, dtype=jnp.int32)[None, :, None]
    in_ids = jnp.arange(span, dtype=jnp.int32)[None, None, :]
    forward_table = (in_ids - out_ids == tap_ids).astype(jnp.float32)
    backward_table = (out_ids + 2 * halo - in_ids == tap_ids).astype(jnp.float32)
    forward_band = band_matrix(window[:, :, :, reach : reach + rows_here], forward_table)
    backward_rows = jnp.stack(
        [
            window[:, taps_lat - 1 - offset, :, offset : offset + rows_here]
            for offset in range(taps_lat)
        ],
        axis=1,
    )
    backward_band = band_matrix(backward_rows, backward_table)
    filtered = apply_band(forward_band, extend_lat(features, reach), halo, rows_here, taps_lat)
    flat = filtered.astype(jnp.bfloat16).reshape(rows_here * width_here, kernels * channels)
    pre = jnp.dot(flat, mixing, preferred_element_type=jnp.float32) + channel_bias
    cell_grads = cotangent.reshape(rows_here * width_here, channels).astype(jnp.float32)
    _, pullback = jax.vjp(gelu_exact, pre)
    (grad_pre,) = pullback(cell_grads)
    grad_pre = grad_pre.astype(jnp.bfloat16)
    local_sum = lax.dot_general(
        flat, grad_pre, (((0,), (0,)), ((), ())), preferred_element_type=jnp.float32
    )
    cell_count = rows_here * lax.axis_size("lat") * width_here * lax.axis_size("lon")
    total = lax.psum(local_sum, ("lon", "lat"))
    mixing_grad = (total / math.sqrt(cell_count)).astype(jnp.bfloat16)
    grad_grid = grad_pre.reshape(rows_here, width_here, channels)
    spread = apply_band(backward_band, extend_lat(grad_grid, reach), halo, rows_here, taps_lat)
    transposed = (
        mixing.reshape(kernels, channels, channels)
        .transpose(0, 2, 1)
        .reshape(kernels * channels, channels)
    )
    branch = jnp.dot(
        spread.astype(jnp.bfloat16).reshape(rows_here * width_here, kernels * channels),
        transposed,
        preferred_element_type=jnp.float32,
    )
    input_grad = (cell_grads + branch).astype(jnp.bfloat16).reshape(rows_here, width_here, channels)
    return (input_grad, mixing_grad)


def solution(mesh):
    return jax.shard_map(
        per_device,
        mesh=mesh,
        in_specs=(P("lat", "lon", None), P(), P(), P(), P(), P("lat", "lon", None)),
        out_specs=(P("lat", "lon", None), P()),
        check_vma=False,
    )
```

profile of v0, /device:TPU:1, one launch (start us, length us, event | category | flops | bytes accessed | tf_op | source)
XLA Modules:
  0.0 398.6 jit_solution(11968619357974466405)
XLA Ops:
  8.6 6.0 %collective-permute-start = (bf16[2,16,384]{2,1,0:T(8,128)(2,1)}, bf16[2,16,384]{2,1,0:T(8,128)(2,1)S(1)}, u32[]{:S(2)}, u32[]{:S(2)}) collective-permute-start(bf16[2,16,384]{2,1,0:T(8,128)(2,1)} %get-tuple-element.9), channel_id=1, source_target_pairs={{0,1},{1,2},{2,3},{4,5},{5,6},{6,7},{8,9},{9,10},{10,11},{12,13},{... | collective-permute-start | bytes 73736 | tf_op jit(solution)/shard_map/ppermute | solution.py:16
  14.6 4.0 %collective-permute-start.1 = (bf16[2,16,384]{2,1,0:T(8,128)(2,1)}, bf16[2,16,384]{2,1,0:T(8,128)(2,1)S(1)}, u32[]{:S(2)}, u32[]{:S(2)}) collective-permute-start(bf16[2,16,384]{2,1,0:T(8,128)(2,1)} %get-tuple-element.8), channel_id=1, source_target_pairs={{1,0},{2,1},{3,2},{5,4},{6,5},{7,6},{9,8},{10,9},{11,10},{13,12},{... | collective-permute-start | bytes 73736 | tf_op jit(solution)/shard_map/ppermute | solution.py:19
  21.2 1.8 convolution_convert_fusion.2
  23.7 3.7 copy.20
  27.7 1.9 collective-permute-start.2
  29.6 11.5 %collective-permute-start.3 = (bf16[84,8,384]{2,1,0:T(8,128)(2,1)S(1)}, bf16[84,8,384]{2,1,0:T(8,128)(2,1)S(1)}, u32[]{:S(2)}, u32[]{:S(2)}) collective-permute-start(bf16[84,8,384]{2,1,0:T(8,128)(2,1)S(1)} %get-tuple-element.5), channel_id=1, source_target_pairs={{4,0},{8,4},{12,8},{16,12},{20,16},{24,20},{28,24},{32,28},{36,32}... | collective-permute-start | bytes 1548296 | tf_op jit(solution)/shard_map/ppermute | solution.py:19
  42.6 6.2 %collective-permute-done.2 = bf16[84,8,384]{2,1,0:T(8,128)(2,1)S(1)} collective-permute-done((bf16[84,8,384]{2,1,0:T(8,128)(2,1)S(1)}, bf16[84,8,384]{2,1,0:T(8,128)(2,1)S(1)}, u32[]{:S(2)}, u32[]{:S(2)}) %collective-permute-start.2) | collective-permute-done | bytes 516128 | tf_op jit(solution)/shard_map/ppermute | solution.py:16
  48.9 1.8 collective-permute-done.3
  50.9 1.5 fusion.18
  52.3 1.6 fusion.17
  56.8 1.5 fusion.14
  58.3 8.6 %copy.19 = bf16[80,5,32,384]{3,2,1,0:T(8,128)(2,1)} copy(bf16[80,5,32,384]{3,2,0,1:T(8,128)(2,1)} %fusion.14) | data formatting | bytes 19660800 | tf_op jit(solution)/shard_map/stack | solution.py:45
  66.9 6.3 %convolution_convert_fusion.1 = bf16[80,48,384]{2,1,0:T(8,128)(2,1)S(1)} fusion(bf16[80,48,160]{2,1,0:T(8,128)(2,1)} %copy.20, bf16[80,160,384]{2,1,0:T(8,128)(2,1)} %bitcast.84), kind=kOutput, calls=%fused_computation.7 | convolution fusion | flops 473333760 | bytes 14008320 | tf_op jit(solution)/shard_map/anm,amc->anc/dot_general | solution.py:50
  73.2 3.3 reshape.116
  76.5 8.2 %fusion.7 = bf16[1280,384]{1,0:T(8,128)(2,1)S(1)} fusion(bf16[1280,384]{1,0:T(8,128)(2,1)} %bitcast.94, bf16[1280,1152]{1,0:T(8,128)(2,1)} %reshape.116, bf16[1152,384]{1,0:T(8,128)(2,1)} %param.9, f32[384]{0:T(512)S(1)} %copy-done.1), kind=kOutput, calls=%fused_computation.16 | convolution fusion | flops 1168834560 | bytes 5801472 | tf_op jit(solution)/shard_map/dot_general | solution.py:86
  84.7 5.0 %collective-permute-start.4 = (bf16[2,16,384]{2,1,0:T(8,128)(2,1)S(1)}, bf16[2,16,384]{2,1,0:T(8,128)(2,1)S(1)}, u32[]{:S(2)}, u32[]{:S(2)}) collective-permute-start(bf16[2,16,384]{2,1,0:T(8,128)(2,1)S(1)} %bitcast.93), channel_id=1, source_target_pairs={{0,1},{1,2},{2,3},{4,5},{5,6},{6,7},{8,9},{9,10},{10,11},{12,13},{... | collective-permute-start | bytes 73736 | tf_op jit(solution)/shard_map/ppermute | solution.py:16
  89.7 1.9 collective-permute-start.5
  92.4 4.0 %collective-permute-done.5 = bf16[2,16,384]{2,1,0:T(8,128)(2,1)S(1)} collective-permute-done((bf16[2,16,384]{2,1,0:T(8,128)(2,1)S(1)}, bf16[2,16,384]{2,1,0:T(8,128)(2,1)S(1)}, u32[]{:S(2)}, u32[]{:S(2)}) %collective-permute-start.5) | collective-permute-done | bytes 24608 | tf_op jit(solution)/shard_map/ppermute | solution.py:19
  97.4 1.9 collective-permute-start.6
  99.3 8.2 %collective-permute-start.7 = (bf16[84,8,384]{2,1,0:T(8,128)(2,1)S(1)}, bf16[84,8,384]{2,1,0:T(8,128)(2,1)}, u32[]{:S(2)}, u32[]{:S(2)}) collective-permute-start(bf16[84,8,384]{2,1,0:T(8,128)(2,1)S(1)} %get-tuple-element.3), channel_id=1, source_target_pairs={{4,0},{8,4},{12,8},{16,12},{20,16},{24,20},{28,24},{32,28},{36,32}... | collective-permute-start | bytes 1548296 | tf_op jit(solution)/shard_map/ppermute | solution.py:19
  107.5 2.7 convolution_convert_fusion.3
  110.2 3.7 copy.22
  113.9 2.3 copy.23
  116.2 4.8 %fusion.41 = f32[1152,384]{1,0:T(8,128)} fusion(bf16[1280,1152]{1,0:T(8,128)(2,1)} %reshape.116, bf16[1280,384]{1,0:T(8,128)(2,1)S(1)} %fusion.7), kind=kOutput, calls=%fused_computation.91 | convolution fusion | flops 1132462080 | bytes 5701632 | tf_op jit(solution)/shard_map/dot_general | solution.py:91
  123.9 1.6 fusion.12
  128.4 1.5 fusion.9
  130.0 8.6 %copy.21 = bf16[80,5,32,384]{3,2,1,0:T(8,128)(2,1)} copy(bf16[80,5,32,384]{3,2,0,1:T(8,128)(2,1)} %fusion.9) | data formatting | bytes 19660800 | tf_op jit(solution)/shard_map/stack | solution.py:45
  138.5 6.3 %convolution_convert_fusion = bf16[80,48,384]{2,1,0:T(8,128)(2,1)S(1)} fusion(bf16[80,48,160]{2,1,0:T(8,128)(2,1)} %copy.22, bf16[80,160,384]{2,1,0:T(8,128)(2,1)} %bitcast.85), kind=kOutput, calls=%fused_computation.6 | convolution fusion | flops 473333760 | bytes 14008320 | tf_op jit(solution)/shard_map/anm,amc->anc/dot_general | solution.py:50
  144.8 3.3 reshape.119
  148.1 5.1 %fusion = bf16[1280,384]{1,0:T(8,128)(2,1)} fusion(bf16[1280,1152]{1,0:T(8,128)(2,1)} %reshape.119, bf16[1152,384]{1,0:T(8,128)(2,1)} %bitcast.91, bf16[1280,384]{1,0:T(8,128)(2,1)} %bitcast.95), kind=kOutput, calls=%fused_computation.5 | convolution fusion | flops 1133936640 | bytes 5799936 | tf_op jit(solution)/shard_map/dot_general | solution.py:104
  153.2 236.0 %all-reduce.3.cloned.1.call-done = f32[1152,384]{1,0:T(8,128)} async-done(((f32[1152,384]{1,0:T(8,128)}), f32[1152,384]{1,0:T(8,128)}) %all-reduce.3.cloned.1.call-update) | async-done | bytes 1769488 | tf_op jit(solution)/shard_map/psum | solution.py:95
  389.2 2.6 multiply_convert_fusion
  (37 shorter events, 17.1 us)
Async XLA Ops:
  7.2 382.0 %all-reduce.3.cloned.1.call-start = ((), (), s32[]{:S(2)}) async-start(), calls=%async_computation | async-start | bytes 3538944 | tf_op jit(solution)/shard_map/psum | solution.py:95
  8.6 18.8 %collective-permute-start = (bf16[2,16,384]{2,1,0:T(8,128)(2,1)}, bf16[2,16,384]{2,1,0:T(8,128)(2,1)S(1)}, u32[]{:S(2)}, u32[]{:S(2)}) collective-permute-start(bf16[2,16,384]{2,1,0:T(8,128)(2,1)} %get-tuple-element.9), channel_id=1, source_target_pairs={{0,1},{1,2},{2,3},{4,5},{5,6},{6,7},{8,9},{9,10},{10,11},{12,13},{... | collective-permute-start | bytes 73736 | tf_op jit(solution)/shard_map/ppermute | solution.py:16
  14.6 13.0 %collective-permute-start.1 = (bf16[2,16,384]{2,1,0:T(8,128)(2,1)}, bf16[2,16,384]{2,1,0:T(8,128)(2,1)S(1)}, u32[]{:S(2)}, u32[]{:S(2)}) collective-permute-start(bf16[2,16,384]{2,1,0:T(8,128)(2,1)} %get-tuple-element.8), channel_id=1, source_target_pairs={{1,0},{2,1},{3,2},{5,4},{6,5},{7,6},{9,8},{10,9},{11,10},{13,12},{... | collective-permute-start | bytes 73736 | tf_op jit(solution)/shard_map/ppermute | solution.py:19
  23.7 3.7 copy-start
  27.7 21.1 %collective-permute-start.2 = (bf16[84,8,384]{2,1,0:T(8,128)(2,1)S(1)}, bf16[84,8,384]{2,1,0:T(8,128)(2,1)S(1)}, u32[]{:S(2)}, u32[]{:S(2)}) collective-permute-start(bf16[84,8,384]{2,1,0:T(8,128)(2,1)S(1)} %get-tuple-element.4), channel_id=1, source_target_pairs={{0,4},{4,8},{8,12},{12,16},{16,20},{20,24},{24,28},{28,32},{32,36}... | collective-permute-start | bytes 1548296 | tf_op jit(solution)/shard_map/ppermute | solution.py:16
  29.6 21.0 %collective-permute-start.3 = (bf16[84,8,384]{2,1,0:T(8,128)(2,1)S(1)}, bf16[84,8,384]{2,1,0:T(8,128)(2,1)S(1)}, u32[]{:S(2)}, u32[]{:S(2)}) collective-permute-start(bf16[84,8,384]{2,1,0:T(8,128)(2,1)S(1)} %get-tuple-element.5), channel_id=1, source_target_pairs={{4,0},{8,4},{12,8},{16,12},{20,16},{24,20},{28,24},{32,28},{36,32}... | collective-permute-start | bytes 1548296 | tf_op jit(solution)/shard_map/ppermute | solution.py:19
  73.2 3.3 copy-start.1
  84.7 7.6 %collective-permute-start.4 = (bf16[2,16,384]{2,1,0:T(8,128)(2,1)S(1)}, bf16[2,16,384]{2,1,0:T(8,128)(2,1)S(1)}, u32[]{:S(2)}, u32[]{:S(2)}) collective-permute-start(bf16[2,16,384]{2,1,0:T(8,128)(2,1)S(1)} %bitcast.93), channel_id=1, source_target_pairs={{0,1},{1,2},{2,3},{4,5},{5,6},{6,7},{8,9},{9,10},{10,11},{12,13},{... | collective-permute-start | bytes 73736 | tf_op jit(solution)/shard_map/ppermute | solution.py:16
  89.7 6.7 %collective-permute-start.5 = (bf16[2,16,384]{2,1,0:T(8,128)(2,1)S(1)}, bf16[2,16,384]{2,1,0:T(8,128)(2,1)S(1)}, u32[]{:S(2)}, u32[]{:S(2)}) collective-permute-start(bf16[2,16,384]{2,1,0:T(8,128)(2,1)S(1)} %bitcast.92), channel_id=1, source_target_pairs={{1,0},{2,1},{3,2},{5,4},{6,5},{7,6},{9,8},{10,9},{11,10},{13,12},{... | collective-permute-start | bytes 73736 | tf_op jit(solution)/shard_map/ppermute | solution.py:19
  97.4 23.6 %collective-permute-start.6 = (bf16[84,8,384]{2,1,0:T(8,128)(2,1)}, bf16[84,8,384]{2,1,0:T(8,128)(2,1)}, u32[]{:S(2)}, u32[]{:S(2)}) collective-permute-start(bf16[84,8,384]{2,1,0:T(8,128)(2,1)} %get-tuple-element.2), channel_id=1, source_target_pairs={{0,4},{4,8},{8,12},{12,16},{16,20},{20,24},{24,28},{28,32},{32,36}... | collective-permute-start | bytes 1548296 | tf_op jit(solution)/shard_map/ppermute | solution.py:16
  99.3 21.7 %collective-permute-start.7 = (bf16[84,8,384]{2,1,0:T(8,128)(2,1)S(1)}, bf16[84,8,384]{2,1,0:T(8,128)(2,1)}, u32[]{:S(2)}, u32[]{:S(2)}) collective-permute-start(bf16[84,8,384]{2,1,0:T(8,128)(2,1)S(1)} %get-tuple-element.3), channel_id=1, source_target_pairs={{4,0},{8,4},{12,8},{16,12},{20,16},{24,20},{28,24},{32,28},{36,32}... | collective-permute-start | bytes 1548296 | tf_op jit(solution)/shard_map/ppermute | solution.py:19
Sparse Core Ops, SparseCore 0:
  121.1 268.0 all-reduce.2
where the time goes:
time: 399 us
  waiting for transfers between devices  248 us (62%)
  local copies, waits for them, and re-layouts  54.5 us (14%)
  starting transfers between devices  40.5 us (10%)
  matrix products  35.2 us (9%)
  between operations  14.3 us (4%)
  other arithmetic  6.19 us (2%)
    psum x1, waiting for transfers between devices, per_device(): total = lax.psum(local_sum, ('lon', 'lat'))  236 us
    ppermute x4, starting transfers between devices, extended_2(): lax.ppermute(lax.slice_in_dim(block, 0, width, axis=dim), axis, backward)  25.6 us
    another operation x4, local copies, waits for them, and re-layouts, stacked_rows(): stacked = jnp.stack(pieces, axis=1)  20.1 us
    unnamed x18, local copies, waits for them, and re-layouts  15 us
    ppermute x4, starting transfers between devices, extended_2(): lax.ppermute(lax.slice_in_dim(block, block.shape[dim] - width, None, axis...  14.8 us
    dot_general x2, matrix products, contract(): jnp.einsum('anm,amc->anc', band, windows, preferred_element_type=jnp.floa...  12.6 us
    dot_general x1, matrix products, per_device(): jnp.dot(flat, mixing, preferred_element_type=jnp.float32) + channel_bias  8.23 us
  transfers between devices with their start and end apart: 9, of which 4 were waited for; matrix products, arithmetic and copies ran while one was open for 14% of the time, Pallas kernels for 0%

commit v1 on v0

--- a/solution.py
+++ b/solution.py
@@ -3,7 +3,194 @@
 import jax
 import jax.numpy as jnp
 from jax import lax
+from jax.experimental import pallas as pl
+from jax.experimental.pallas import tpu as pltpu
 from jax.sharding import PartitionSpec as P
+
+MESH = pl.DeviceIdType.MESH
+SIZE_X_LO, SIZE_Z, SIZE_Y = 2, 8, 8
+SIZE_X = 4
+
+
+def position():
+    lon, lat = lax.axis_index("lon"), lax.axis_index("lat")
+    x = lax.div(lat, 2) * SIZE_X_LO + lax.div(lon, SIZE_Z * SIZE_Y)
+    z = lax.rem(lax.div(lon, SIZE_Y), SIZE_Z)
+    return x, z, lax.rem(lon, SIZE_Y), lax.rem(lat, 2)
+
+
+def device(x, z, y, core):
+    lon = (lax.rem(x, SIZE_X_LO) * SIZE_Z + z) * SIZE_Y + y
+    return {"lon": lon, "lat": lax.div(x, SIZE_X_LO) * 2 + core}
+
+
+def sum_peers():
+    x, z, y, core = position()
+    peers = [device(x, z, y, 1 - core)]
+    peers += [device(lax.rem(x + d, SIZE_X), z, y, core) for d in range(1, SIZE_X)]
+    peers += [device(x, lax.rem(z + d, SIZE_Z), y, core) for d in range(1, SIZE_Z)]
+    peers += [device(x, z, lax.rem(y + d, SIZE_Y), core) for d in range(1, SIZE_Y)]
+    return peers
+
+
+def greet(peers):
+    barrier = pltpu.get_barrier_semaphore()
+    for peer in peers:
+        pl.semaphore_signal(barrier, inc=1, device_id=peer, device_id_type=MESH)
+    pl.semaphore_wait(barrier, len(peers))
+
+
+def sum_buffers(part_rows, channels):
+    tiles = (part_rows // 16) * (channels // 128)
+    share = -(-tiles // SIZE_Z)
+    copies = 2 + 2 * (SIZE_X - 1) + 2 * (SIZE_Z - 1) + SIZE_Y - 1
+    return [
+        pltpu.VMEM((SIZE_X, part_rows, channels), jnp.float32),
+        pltpu.VMEM((SIZE_X, part_rows, channels), jnp.bfloat16),
+        pltpu.VMEM((SIZE_X - 1, part_rows, channels), jnp.bfloat16),
+        pltpu.VMEM((SIZE_Z, share, 16, 128), jnp.float32),
+        pltpu.VMEM((SIZE_Z, share, 16, 128), jnp.bfloat16),
+        pltpu.VMEM((SIZE_Z - 1, share, 16, 128), jnp.bfloat16),
+        pltpu.VMEM((SIZE_Y, share, 16, 128), jnp.bfloat16),
+        pltpu.VMEM((SIZE_Z, share, 16, 128), jnp.bfloat16),
+        pltpu.VMEM((2, SIZE_X, part_rows, channels), jnp.bfloat16),
+        pltpu.SemaphoreType.DMA((copies,)),
+        pltpu.SemaphoreType.DMA((copies,)),
+    ]
+
+
+class SumOverAll:
+    def __init__(self, local, buffers, scale):
+        self.local, self.scale = local, scale
+        (self.half, self.x_out, self.x_in, self.z_own, self.z_out, self.z_in, self.y_all, self.z_done, self.done,
+         self.send, self.recv) = buffers
+        self.x, self.z, self.y, self.core = position()
+        self.used = 0
+        self.rows, self.channels = local.shape[2:]
+        self.lanes = self.channels // 128
+        self.tiles = (self.rows // 16) * self.lanes
+        self.share = self.z_own.shape[1]
+
+    def copy(self, src, dst, peer):
+        index = self.used
+        self.used += 1
+        copy = pltpu.make_async_remote_copy(
+            src_ref=src, dst_ref=dst, send_sem=self.send.at[index], recv_sem=self.recv.at[index],
+            device_id=peer, device_id_type=MESH)
+        copy.start()
+        return copy
+
+    def tile(self, t):
+        row, lane = t // self.lanes * 16, t % self.lanes * 128
+        return slice(row, row + 16), slice(lane, lane + 128)
+
+    def start_core(self):
+        self.flying = [self.copy(self.local.at[1 - self.core], self.half, device(self.x, self.z, self.y, 1 - self.core))]
+
+    def wait(self):
+        for copy in self.flying:
+            copy.wait()
+
+    def finish_core_start_x(self):
+        self.wait()
+        for part in range(SIZE_X):
+            total = self.half[part] + self.local[self.core, part]
+            self.half[part] = total
+            self.x_out[part] = total.astype(jnp.bfloat16)
+        self.flying = []
+        for d in range(1, SIZE_X):
+            peer = lax.rem(self.x + d, SIZE_X)
+            self.flying.append(self.copy(self.x_out.at[peer], self.x_in.at[d - 1], device(peer, self.z, self.y, self.core)))
+
+    def finish_x_start_z(self):
+        self.wait()
+        for t in range(SIZE_Z * self.share):
+            group, slot = t // self.share, t % self.share
+            if t < self.tiles:
+                rows, lanes = self.tile(t)
+                total = self.half[self.x, rows, lanes]
+                for d in range(1, SIZE_X):
+                    total = total + self.x_in[d - 1, rows, lanes].astype(jnp.float32)
+            else:
+                total = jnp.zeros((16, 128), jnp.float32)
+            self.z_own[group, slot] = total
+            self.z_out[group, slot] = total.astype(jnp.bfloat16)
+        self.flying = []
+        for d in range(1, SIZE_Z):
+            peer = lax.rem(self.z + d, SIZE_Z)
+            self.flying.append(self.copy(self.z_out.at[peer], self.z_in.at[d - 1], device(self.x, peer, self.y, self.core)))
+
+    def finish_z_start_y(self):
+        self.wait()
+        total = self.z_own[self.z]
+        for d in range(1, SIZE_Z):
+            total = total + self.z_in[d - 1].astype(jnp.float32)
+        self.y_all[self.y] = total.astype(jnp.bfloat16)
+        self.flying = []
+        for d in range(1, SIZE_Y):
+            peer = lax.rem(self.y + d, SIZE_Y)
+            self.flying.append(self.copy(self.y_all.at[self.y], self.y_all.at[self.y], device(self.x, self.z, peer, self.core)))
+
+    def finish_y_start_gather(self):
+        self.wait()
+        total = self.y_all[0].astype(jnp.float32)
+        for other in range(1, SIZE_Y):
+            total = total + self.y_all[other].astype(jnp.float32)
+        self.z_done[self.z] = (total / self.scale).astype(jnp.bfloat16)
+        self.flying = []
+        for d in range(1, SIZE_Z):
+            peer = lax.rem(self.z + d, SIZE_Z)
+            self.flying.append(self.copy(self.z_done.at[self.z], self.z_done.at[self.z], device(self.x, peer, self.y, self.core)))
+
+    def finish_z_gather_x(self):
+        self.wait()
+        for t in range(self.tiles):
+            rows, lanes = self.tile(t)
+            self.done[self.core, self.x, rows, lanes] = self.z_done[t // self.share, t % self.share]
+        self.flying = []
+        block = self.done.at[self.core, self.x]
+        for d in range(1, SIZE_X):
+            peer = lax.rem(self.x + d, SIZE_X)
+            self.flying.append(self.copy(block, block, device(peer, self.z, self.y, self.core)))
+
+    def finish_x_gather_core(self):
+        self.wait()
+        block = self.done.at[self.core]
+        self.flying = [self.copy(block, block, device(self.x, self.z, self.y, 1 - self.core))]
+
+    def finish(self, out):
+        self.wait()
+        for core in range(2):
+            for part in range(SIZE_X):
+                at = (core * SIZE_X + part) * self.rows
+                out[at : at + self.rows, :] = self.done[core, part]
+
+
+def sum_kernel(scale, local, out, *buffers):
+    greet(sum_peers())
+    work = SumOverAll(local, buffers, scale)
+    work.start_core()
+    work.finish_core_start_x()
+    work.finish_x_start_z()
+    work.finish_z_start_y()
+    work.finish_y_start_gather()
+    work.finish_z_gather_x()
+    work.finish_x_gather_core()
+    work.finish(out)
+
+
+def sum_over_all(local, scale):
+    rows, channels = local.shape
+    part_rows = rows // (2 * SIZE_X)
+    return pl.pallas_call(
+        lambda *refs: sum_kernel(scale, *refs),
+        out_shape=jax.ShapeDtypeStruct((rows, channels), jnp.bfloat16),
+        in_specs=[pl.BlockSpec(memory_space=pltpu.VMEM)],
+        out_specs=pl.BlockSpec(memory_space=pltpu.VMEM),
+        scratch_shapes=sum_buffers(part_rows, channels),
+        compiler_params=pltpu.CompilerParams(
+            collective_id=0, has_side_effects=True, vmem_limit_bytes=32 * 1024 * 1024),
+    )(local.reshape(2, SIZE_X, part_rows, channels))
 
 
 def extended_2(block, sides, width, periodic):
@@ -92,8 +279,7 @@
         flat, grad_pre, (((0,), (0,)), ((), ())), preferred_element_type=jnp.float32
     )
     cell_count = rows_here * lax.axis_size("lat") * width_here * lax.axis_size("lon")
-    total = lax.psum(local_sum, ("lon", "lat"))
-    mixing_grad = (total / math.sqrt(cell_count)).astype(jnp.bfloat16)
+    mixing_grad = sum_over_all(local_sum, math.sqrt(cell_count))
     grad_grid = grad_pre.reshape(rows_here, width_here, channels)
     spread = apply_band(backward_band, extend_lat(grad_grid, reach), halo, rows_here, taps_lat)
     transposed = (

time: 399 us -> 196 us (0.49)
  waiting for transfers between devices: 248 us -> 12 us
  Pallas kernels: 0 us -> 38.8 us
  between operations: 14.3 us -> 0.9 us
  local copies, waits for them, and re-layouts: 54.5 us -> 63.6 us
    psum x1 -> x0, waiting for transfers between devices: 236 us -> none  [per_device(): total = lax.psum(local_sum, ('lon', 'lat'))]
    pallas_call x0 -> x1, Pallas kernels: none -> 38.8 us  [sum_over_all(): pl.pallas_call(lambda *refs: sum_kernel(scale, *refs), out_shape=jax.Shap...]
    dot_general x0 -> x1, local copies, waits for them, and re-layouts: none -> 5.45 us  [per_device(): lax.dot_general(flat, grad_pre, (((0,), (0,)), ((), ())), preferred_eleme...]
    unnamed x18 -> x29, local copies, waits for them, and re-layouts: 15 us -> 15.9 us
  transfers between devices with their start and end apart: 9 -> 8, of which waited for: 4 -> 3; matrix products, arithmetic and copies ran while one was open for 14% -> 16% of each run, Pallas kernels for 0% -> 20%
where the time goes in v1:
time: 196 us; the launch traced here: 195 us
  local copies, waits for them, and re-layouts  63.6 us (32%)
  starting transfers between devices  40.5 us (21%)
  Pallas kernels  38.8 us (20%)
  matrix products  35.8 us (18%)
  waiting for transfers between devices  12 us (6%)
  other arithmetic  3.63 us (2%)
    pallas_call x1, Pallas kernels, sum_over_all(): pl.pallas_call(lambda *refs: sum_kernel(scale, *refs), out_shape=jax.Shap...  38.8 us
    ppermute x4, starting transfers between devices, extended_2(): lax.ppermute(lax.slice_in_dim(block, 0, width, axis=dim), axis, backward)  25.6 us
    another operation x4, local copies, waits for them, and re-layouts, stacked_rows(): stacked = jnp.stack(pieces, axis=1)  20.1 us
    unnamed x29, local copies, waits for them, and re-layouts  15.9 us
    ppermute x4, starting transfers between devices, extended_2(): lax.ppermute(lax.slice_in_dim(block, block.shape[dim] - width, None, axis...  14.8 us
    dot_general x2, matrix products, contract(): jnp.einsum('anm,amc->anc', band, windows, preferred_element_type=jnp.floa...  13.5 us
    dot_general x1, matrix products, per_device(): jnp.dot(flat, mixing, preferred_element_type=jnp.float32) + channel_bias  8.23 us
    convert_element_type x2, local copies, waits for them, and re-layouts, band_matrix(): band.reshape(count_rows, width_out * kernels, taps_lat * width_in)  7.72 us
  transfers between devices with their start and end apart: 8, of which 3 were waited for; matrix products, arithmetic and copies ran while one was open for 16% of the time, Pallas kernels for 20%

profile of v1, /device:TPU:1, one launch (start us, length us, event | category | flops | bytes accessed | tf_op | source)
XLA Modules:
  0.0 195.1 jit_solution(3547841208722563890)
XLA Ops:
  2.0 6.0 %collective-permute-start = (bf16[2,16,384]{2,1,0:T(8,128)(2,1)}, bf16[2,16,384]{2,1,0:T(8,128)(2,1)S(1)}, u32[]{:S(2)}, u32[]{:S(2)}) collective-permute-start(bf16[2,16,384]{2,1,0:T(8,128)(2,1)} %get-tuple-element.9), channel_id=1, source_target_pairs={{0,1},{1,2},{2,3},{4,5},{5,6},{6,7},{8,9},{9,10},{10,11},{12,13},{... | collective-permute-start | bytes 73736 | tf_op jit(solution)/shard_map/ppermute | solution.py:203
  8.0 4.0 %collective-permute-start.1 = (bf16[2,16,384]{2,1,0:T(8,128)(2,1)}, bf16[2,16,384]{2,1,0:T(8,128)(2,1)S(1)}, u32[]{:S(2)}, u32[]{:S(2)}) collective-permute-start(bf16[2,16,384]{2,1,0:T(8,128)(2,1)} %get-tuple-element.8), channel_id=1, source_target_pairs={{1,0},{2,1},{3,2},{5,4},{6,5},{7,6},{9,8},{10,9},{11,10},{13,12},{... | collective-permute-start | bytes 73736 | tf_op jit(solution)/shard_map/ppermute | solution.py:206
  14.6 1.8 convolution_convert_fusion.2
  17.1 3.7 %copy.22 = bf16[80,48,160]{2,1,0:T(8,128)(2,1)} copy(bf16[80,48,160]{0,2,1:T(8,128)(2,1)S(1)} %bitcast.93) | data formatting | bytes 2457600 | tf_op jit(solution)/shard_map/convert_element_type | solution.py:227
  21.1 1.9 collective-permute-start.2
  23.1 11.5 %collective-permute-start.3 = (bf16[84,8,384]{2,1,0:T(8,128)(2,1)S(1)}, bf16[84,8,384]{2,1,0:T(8,128)(2,1)S(1)}, u32[]{:S(2)}, u32[]{:S(2)}) collective-permute-start(bf16[84,8,384]{2,1,0:T(8,128)(2,1)S(1)} %get-tuple-element.5), channel_id=1, source_target_pairs={{4,0},{8,4},{12,8},{16,12},{20,16},{24,20},{28,24},{32,28},{36,32}... | collective-permute-start | bytes 1548296 | tf_op jit(solution)/shard_map/ppermute | solution.py:206
  36.1 6.2 %collective-permute-done.2 = bf16[84,8,384]{2,1,0:T(8,128)(2,1)S(1)} collective-permute-done((bf16[84,8,384]{2,1,0:T(8,128)(2,1)S(1)}, bf16[84,8,384]{2,1,0:T(8,128)(2,1)S(1)}, u32[]{:S(2)}, u32[]{:S(2)}) %collective-permute-start.2) | collective-permute-done | bytes 516128 | tf_op jit(solution)/shard_map/ppermute | solution.py:203
  42.3 1.8 collective-permute-done.3
  44.3 1.5 fusion.18
  45.7 1.6 fusion.17
  50.2 1.5 fusion.14
  51.7 8.5 %copy.21 = bf16[80,5,32,384]{3,2,1,0:T(8,128)(2,1)} copy(bf16[80,5,32,384]{3,2,0,1:T(8,128)(2,1)} %fusion.14) | data formatting | bytes 19660800 | tf_op jit(solution)/shard_map/stack | solution.py:232
  60.3 6.3 %convolution_convert_fusion.1 = bf16[80,48,384]{2,1,0:T(8,128)(2,1)S(1)} fusion(bf16[80,48,160]{2,1,0:T(8,128)(2,1)} %copy.22, bf16[80,160,384]{2,1,0:T(8,128)(2,1)} %bitcast.90), kind=kOutput, calls=%fused_computation.7 | convolution fusion | flops 473333760 | bytes 14008320 | tf_op jit(solution)/shard_map/anm,amc->anc/dot_general | solution.py:237
  66.6 3.3 %reshape.118 = bf16[1280,1152]{1,0:T(8,128)(2,1)} reshape(bf16[80,48,384]{2,1,0:T(8,128)(2,1)S(1)} %convolution_convert_fusion.1) | data formatting | bytes 5898240 | tf_op jit(solution)/shard_map/reshape | solution.py:272
  69.9 8.2 %fusion.7 = bf16[1280,384]{1,0:T(8,128)(2,1)S(1)} fusion(bf16[1280,384]{1,0:T(8,128)(2,1)} %bitcast.102, bf16[1280,1152]{1,0:T(8,128)(2,1)} %reshape.118, bf16[1152,384]{1,0:T(8,128)(2,1)} %param.9, f32[384]{0:T(512)S(1)} %copy-done.6), kind=kOutput, calls=%fused_computation.16 | convolution fusion | flops 1168834560 | bytes 5801472 | tf_op jit(solution)/shard_map/dot_general | solution.py:273
  78.2 5.0 %collective-permute-start.4 = (bf16[2,16,384]{2,1,0:T(8,128)(2,1)S(1)}, bf16[2,16,384]{2,1,0:T(8,128)(2,1)S(1)}, u32[]{:S(2)}, u32[]{:S(2)}) collective-permute-start(bf16[2,16,384]{2,1,0:T(8,128)(2,1)S(1)} %bitcast.101), channel_id=1, source_target_pairs={{0,1},{1,2},{2,3},{4,5},{5,6},{6,7},{8,9},{9,10},{10,11},{12,13},{... | collective-permute-start | bytes 73736 | tf_op jit(solution)/shard_map/ppermute | solution.py:203
  83.2 1.9 collective-permute-start.5
  85.8 4.0 %collective-permute-done.5 = bf16[2,16,384]{2,1,0:T(8,128)(2,1)S(1)} collective-permute-done((bf16[2,16,384]{2,1,0:T(8,128)(2,1)S(1)}, bf16[2,16,384]{2,1,0:T(8,128)(2,1)S(1)}, u32[]{:S(2)}, u32[]{:S(2)}) %collective-permute-start.5) | collective-permute-done | bytes 24608 | tf_op jit(solution)/shard_map/ppermute | solution.py:206
  90.9 1.9 collective-permute-start.6
  92.8 8.2 %collective-permute-start.7 = (bf16[84,8,384]{2,1,0:T(8,128)(2,1)S(1)}, bf16[84,8,384]{2,1,0:T(8,128)(2,1)}, u32[]{:S(2)}, u32[]{:S(2)}) collective-permute-start(bf16[84,8,384]{2,1,0:T(8,128)(2,1)S(1)} %get-tuple-element.3), channel_id=1, source_target_pairs={{4,0},{8,4},{12,8},{16,12},{20,16},{24,20},{28,24},{32,28},{36,32}... | collective-permute-start | bytes 1548296 | tf_op jit(solution)/shard_map/ppermute | solution.py:206
  101.0 3.9 %convolution_convert_fusion.3 = bf16[16,32,3,5,80]{4,1,3,2,0:T(8,128)(2,1)} fusion(f32[3,5,17,80]{3,2,1,0:T(8,128)} %constant_dynamic-update-slice_fusion, s32[16,32]{1,0:T(8,128)S(1)} %iota_subtract_fusion.1), kind=kOutput, calls=%fused_computation.54 | convolution fusion | flops 125960704 | bytes 1312448 | tf_op jit(solution)/shard_map/bsqa,qvu->avbsu/dot_general | solution.py:225
  104.9 4.1 %copy.24 = bf16[80,48,160]{2,1,0:T(8,128)(2,1)S(1)} copy(bf16[80,48,160]{0,2,1:T(8,128)(2,1)} %bitcast.94) | data formatting | bytes 2457600 | tf_op jit(solution)/shard_map/convert_element_type | solution.py:227
  109.0 2.2 %copy.25 = bf16[3,384,384]{2,1,0:T(8,128)(2,1)} copy(bf16[3,384,384]{1,2,0:T(8,128)(2,1)S(1)} %bitcast.98) | data formatting | bytes 1769472 | tf_op jit(solution)/shard_map/transpose | solution.py:287
  111.1 5.5 %copy.26 = bf16[1152,1280]{1,0:T(8,128)(2,1)} copy(bf16[1152,1280]{0,1:T(8,128)(2,1)} %bitcast.92) | data formatting | bytes 5898240 | tf_op jit(solution)/shard_map/dot_general | solution.py:278
  116.6 3.8 %fusion.26.refs_0_ = f32[2,4,144,384]{3,2,1,0:T(8,128)S(1)} fusion(bf16[2,4,144,1280]{3,2,1,0:T(8,128)(2,1)} %bitcast.97, bf16[1280,384]{1,0:T(8,128)(2,1)} %copy-done), kind=kOutput, calls=%fused_computation.56 | convolution fusion | flops 1132462080 | bytes 5701632 | tf_op jit(solution)/shard_map/dot_general | solution.py:278
  120.4 38.8 %shard_map.77 = bf16[1152,384]{1,0:T(8,128)(2,1)S(1)} custom-call(f32[2,4,144,384]{3,2,1,0:T(8,128)S(1)} %fusion.26.refs_0_), custom_call_target="tpu_custom_call" | custom-call | tf_op jit(solution)/shard_map/pallas_call | solution.py:185
  162.1 1.6 fusion.12
  166.6 1.5 fusion.9
  168.1 8.5 %copy.23 = bf16[80,5,32,384]{3,2,1,0:T(8,128)(2,1)} copy(bf16[80,5,32,384]{3,2,0,1:T(8,128)(2,1)} %fusion.9) | data formatting | bytes 19660800 | tf_op jit(solution)/shard_map/stack | solution.py:232
  176.6 7.3 %convolution_convert_fusion = bf16[80,48,384]{2,1,0:T(8,128)(2,1)} fusion(bf16[80,48,160]{2,1,0:T(8,128)(2,1)S(1)} %copy.24, bf16[80,160,384]{2,1,0:T(8,128)(2,1)} %bitcast.91), kind=kOutput, calls=%fused_computation.6 | convolution fusion | flops 473333760 | bytes 14008320 | tf_op jit(solution)/shard_map/anm,amc->anc/dot_general | solution.py:237
  183.9 5.8 %reshape.121 = bf16[1280,1152]{1,0:T(8,128)(2,1)} reshape(bf16[80,48,384]{2,1,0:T(8,128)(2,1)} %convolution_convert_fusion) | data formatting | bytes 5898240 | tf_op jit(solution)/shard_map/reshape | solution.py:291
  189.7 4.6 %fusion = bf16[1280,384]{1,0:T(8,128)(2,1)} fusion(bf16[1280,1152]{1,0:T(8,128)(2,1)} %reshape.121, bf16[1152,384]{1,0:T(8,128)(2,1)S(1)} %bitcast.99, bf16[1280,384]{1,0:T(8,128)(2,1)S(1)} %bitcast.103), kind=kOutput, calls=%fused_computation.5 | convolution fusion | flops 1133936640 | bytes 5799936 | tf_op jit(solution)/shard_map/dot_general | solution.py:290
  (46 shorter events, 18.1 us)
Async XLA Ops:
  2.0 18.8 %collective-permute-start = (bf16[2,16,384]{2,1,0:T(8,128)(2,1)}, bf16[2,16,384]{2,1,0:T(8,128)(2,1)S(1)}, u32[]{:S(2)}, u32[]{:S(2)}) collective-permute-start(bf16[2,16,384]{2,1,0:T(8,128)(2,1)} %get-tuple-element.9), channel_id=1, source_target_pairs={{0,1},{1,2},{2,3},{4,5},{5,6},{6,7},{8,9},{9,10},{10,11},{12,13},{... | collective-permute-start | bytes 73736 | tf_op jit(solution)/shard_map/ppermute | solution.py:203
  8.0 13.0 %collective-permute-start.1 = (bf16[2,16,384]{2,1,0:T(8,128)(2,1)}, bf16[2,16,384]{2,1,0:T(8,128)(2,1)S(1)}, u32[]{:S(2)}, u32[]{:S(2)}) collective-permute-start(bf16[2,16,384]{2,1,0:T(8,128)(2,1)} %get-tuple-element.8), channel_id=1, source_target_pairs={{1,0},{2,1},{3,2},{5,4},{6,5},{7,6},{9,8},{10,9},{11,10},{13,12},{... | collective-permute-start | bytes 73736 | tf_op jit(solution)/shard_map/ppermute | solution.py:206
  17.1 3.7 %copy-start.2 = (bf16[80,16,384]{2,1,0:T(8,128)(2,1)S(1)}, bf16[80,16,384]{2,1,0:T(8,128)(2,1)}, u32[]{:S(2)}) copy-start(bf16[80,16,384]{2,1,0:T(8,128)(2,1)} %param.6) | copy-start | bytes 2949124
  21.1 21.1 %collective-permute-start.2 = (bf16[84,8,384]{2,1,0:T(8,128)(2,1)S(1)}, bf16[84,8,384]{2,1,0:T(8,128)(2,1)S(1)}, u32[]{:S(2)}, u32[]{:S(2)}) collective-permute-start(bf16[84,8,384]{2,1,0:T(8,128)(2,1)S(1)} %get-tuple-element.4), channel_id=1, source_target_pairs={{0,4},{4,8},{8,12},{12,16},{16,20},{20,24},{24,28},{28,32},{32,36}... | collective-permute-start | bytes 1548296 | tf_op jit(solution)/shard_map/ppermute | solution.py:203
  23.1 21.0 %collective-permute-start.3 = (bf16[84,8,384]{2,1,0:T(8,128)(2,1)S(1)}, bf16[84,8,384]{2,1,0:T(8,128)(2,1)S(1)}, u32[]{:S(2)}, u32[]{:S(2)}) collective-permute-start(bf16[84,8,384]{2,1,0:T(8,128)(2,1)S(1)} %get-tuple-element.5), channel_id=1, source_target_pairs={{4,0},{8,4},{12,8},{16,12},{20,16},{24,20},{28,24},{32,28},{36,32}... | collective-permute-start | bytes 1548296 | tf_op jit(solution)/shard_map/ppermute | solution.py:206
  66.5 3.4 %copy-start.6 = (f32[384]{0:T(512)S(1)}, f32[384]{0:T(512)}, u32[]{:S(2)}) copy-start(f32[384]{0:T(512)} %param.10) | copy-start | bytes 4612
  78.1 12.7 %copy-start = (bf16[1280,384]{1,0:T(8,128)(2,1)}, bf16[1280,384]{1,0:T(8,128)(2,1)S(1)}, u32[]{:S(2)}) copy-start(bf16[1280,384]{1,0:T(8,128)(2,1)S(1)} %fusion.7) | copy-start | bytes 2949124
  78.2 7.6 %collective-permute-start.4 = (bf16[2,16,384]{2,1,0:T(8,128)(2,1)S(1)}, bf16[2,16,384]{2,1,0:T(8,128)(2,1)S(1)}, u32[]{:S(2)}, u32[]{:S(2)}) collective-permute-start(bf16[2,16,384]{2,1,0:T(8,128)(2,1)S(1)} %bitcast.101), channel_id=1, source_target_pairs={{0,1},{1,2},{2,3},{4,5},{5,6},{6,7},{8,9},{9,10},{10,11},{12,13},{... | collective-permute-start | bytes 73736 | tf_op jit(solution)/shard_map/ppermute | solution.py:203
  83.2 6.7 %collective-permute-start.5 = (bf16[2,16,384]{2,1,0:T(8,128)(2,1)S(1)}, bf16[2,16,384]{2,1,0:T(8,128)(2,1)S(1)}, u32[]{:S(2)}, u32[]{:S(2)}) collective-permute-start(bf16[2,16,384]{2,1,0:T(8,128)(2,1)S(1)} %bitcast.100), channel_id=1, source_target_pairs={{1,0},{2,1},{3,2},{5,4},{6,5},{7,6},{9,8},{10,9},{11,10},{13,12},{... | collective-permute-start | bytes 73736 | tf_op jit(solution)/shard_map/ppermute | solution.py:206
  90.9 68.3 %collective-permute-start.6 = (bf16[84,8,384]{2,1,0:T(8,128)(2,1)}, bf16[84,8,384]{2,1,0:T(8,128)(2,1)}, u32[]{:S(2)}, u32[]{:S(2)}) collective-permute-start(bf16[84,8,384]{2,1,0:T(8,128)(2,1)} %get-tuple-element.2), channel_id=1, source_target_pairs={{0,4},{4,8},{8,12},{12,16},{16,20},{20,24},{24,28},{28,32},{32,36}... | collective-permute-start | bytes 1548296 | tf_op jit(solution)/shard_map/ppermute | solution.py:203
  92.8 66.4 %collective-permute-start.7 = (bf16[84,8,384]{2,1,0:T(8,128)(2,1)S(1)}, bf16[84,8,384]{2,1,0:T(8,128)(2,1)}, u32[]{:S(2)}, u32[]{:S(2)}) collective-permute-start(bf16[84,8,384]{2,1,0:T(8,128)(2,1)S(1)} %get-tuple-element.3), channel_id=1, source_target_pairs={{4,0},{8,4},{12,8},{16,12},{20,16},{24,20},{28,24},{32,28},{36,32}... | collective-permute-start | bytes 1548296 | tf_op jit(solution)/shard_map/ppermute | solution.py:206
  104.9 4.1 %copy-start.3 = (bf16[1152,384]{1,0:T(8,128)(2,1)S(1)}, bf16[1152,384]{1,0:T(8,128)(2,1)}, u32[]{:S(2)}) copy-start(bf16[1152,384]{1,0:T(8,128)(2,1)} %param.9) | copy-start | bytes 2654212
  120.3 38.8 %copy-start.1 = (bf16[1280,384]{1,0:T(8,128)(2,1)S(1)}, bf16[1280,384]{1,0:T(8,128)(2,1)}, u32[]{:S(2)}) copy-start(bf16[1280,384]{1,0:T(8,128)(2,1)} %copy-done) | copy-start | bytes 2949124
  183.9 5.8 %copy-start.4 = (bf16[3,384,384]{2,1,0:T(8,128)(2,1)S(1)}, bf16[3,384,384]{2,1,0:T(8,128)(2,1)}, u32[]{:S(2)}) copy-start(bf16[3,384,384]{2,1,0:T(8,128)(2,1)} %copy.25) | copy-start | bytes 2654212
  183.9 5.8 %copy-start.5 = (bf16[80,16,384]{2,1,0:T(8,128)(2,1)S(1)}, bf16[80,16,384]{2,1,0:T(8,128)(2,1)}, u32[]{:S(2)}) copy-start(bf16[80,16,384]{2,1,0:T(8,128)(2,1)} %param.11) | copy-start | bytes 2949124

commit v2 on v1

--- a/solution.py
+++ b/solution.py
@@ -166,134 +166,301 @@
                 out[at : at + self.rows, :] = self.done[core, part]
 
 
-def sum_kernel(scale, local, out, *buffers):
-    greet(sum_peers())
-    work = SumOverAll(local, buffers, scale)
-    work.start_core()
-    work.finish_core_start_x()
-    work.finish_x_start_z()
-    work.finish_z_start_y()
-    work.finish_y_start_gather()
+def halo_peers():
+    lon, lat = lax.axis_index("lon"), lax.axis_index("lat")
+    count_lon, count_lat = lax.axis_size("lon"), lax.axis_size("lat")
+    east, west = lax.rem(lon + 1, count_lon), lax.rem(lon + count_lon - 1, count_lon)
+    south, north = lax.rem(lat + 1, count_lat), lax.rem(lat + count_lat - 1, count_lat)
+    return {
+        (row, column): {"lon": at_lon, "lat": at_lat}
+        for row, at_lat in ((-1, north), (0, lat), (1, south))
+        for column, at_lon in ((-1, west), (0, lon), (1, east))
+        if (row, column) != (0, 0)
+    }
+
+
+class Halo:
+    def __init__(self, own, west_in, east_in, west_out, east_out, send, recv, cuts):
+        self.own, self.west_in, self.east_in = own, west_in, east_in
+        self.west_out, self.east_out, self.send, self.recv = west_out, east_out, send, recv
+        self.peers, self.rows, self.cuts, self.used = halo_peers(), own.shape[0] - 4, cuts, 0
+        self.pairs, self.parts, self.top, self.bottom = self.rows // 2, [], [], []
+
+    def copy(self, src, dst, peer):
+        index = self.used
+        self.used += 1
+        copy = pltpu.make_async_remote_copy(
+            src_ref=src, dst_ref=dst, send_sem=self.send.at[index], recv_sem=self.recv.at[index],
+            device_id=self.peers[peer], device_id_type=MESH)
+        copy.start()
+        return copy
+
+    def pack(self, first, values):
+        pairs, channels = values.shape[0] // 2, values.shape[-1]
+        split = values.reshape(pairs, 2, 16, channels)
+        self.west_out[first : first + pairs] = split[:, :, :8].reshape(pairs, 16, channels).astype(jnp.bfloat16)
+        self.east_out[first : first + pairs] = split[:, :, 8:].reshape(pairs, 16, channels).astype(jnp.bfloat16)
+
+    def send_part(self, part):
+        lo, hi = self.cuts[part], self.cuts[part + 1]
+        self.parts.append([
+            self.copy(self.east_out.at[lo:hi], self.west_in.at[lo + 1 : hi + 1], (0, 1)),
+            self.copy(self.west_out.at[lo:hi], self.east_in.at[lo + 1 : hi + 1], (0, -1)),
+        ])
+
+    def send_north(self):
+        rows, last = self.rows, self.pairs + 1
+        self.bottom = [
+            self.copy(self.own.at[2:4], self.own.at[rows + 2 : rows + 4], (-1, 0)),
+            self.copy(self.east_out.at[0:1], self.west_in.at[last : last + 1], (-1, 1)),
+            self.copy(self.west_out.at[0:1], self.east_in.at[last : last + 1], (-1, -1)),
+        ]
+
+    def send_south(self):
+        rows, last = self.rows, self.pairs - 1
+        self.top = [
+            self.copy(self.own.at[rows : rows + 2], self.own.at[0:2], (1, 0)),
+            self.copy(self.east_out.at[last : last + 1], self.west_in.at[0:1], (1, 1)),
+            self.copy(self.west_out.at[last : last + 1], self.east_in.at[0:1], (1, -1)),
+        ]
+
+    def wait(self, copies):
+        for copy in copies:
+            copy.wait()
+
+    def window(self, first):
+        channels = self.own.shape[-1]
+        pair = lax.div(first, 2)
+        return jnp.concatenate([
+            self.own[pl.ds(first, 8)].reshape(128, channels),
+            self.west_in[pl.ds(pair, 4)].reshape(64, channels),
+            self.east_in[pl.ds(pair, 4)].reshape(64, channels),
+        ], axis=0)
+
+
+def iota(shape, dim):
+    return lax.broadcasted_iota(jnp.int32, shape, dim)
+
+
+def lay_taps(filter_basis, half_widths, stage, taps):
+    kernels, taps_lat, taps_lon, rows = filter_basis.shape
+    allowed = jnp.abs(iota((taps_lon, rows), 0) - taps_lon // 2) <= half_widths[...]
+    stage[...] = jnp.zeros_like(stage)
+    taps[...] = jnp.zeros_like(taps)
+    for b in range(kernels):
+        for s in range(taps_lat):
+            values = jnp.where(allowed, filter_basis[b, s].astype(jnp.float32), 0.0)
+            stage[s * 32 : s * 32 + taps_lon, 0:rows] = values
+        taps[b, 8 : 8 + stage.shape[1]] = stage[...].T
+
+
+def base_rows(taps, b, first, rows, total_rows, backward):
+    reach = 2
+    near = taps[b, pl.ds(first, rows + 16)]
+    lane = iota((rows, 256), 1)
+    if not backward:
+        source = iota((rows, 256), 0) + first + lax.div(lane, 32) - reach
+        return jnp.where((source >= 0) & (source < total_rows), near[8 : 8 + rows], 0.0)
+    chosen = jnp.zeros((rows, 256), jnp.float32)
+    for s in range(5):
+        start = 8 + reach - s
+        chosen = jnp.where(lax.div(lane, 32) == s, near[start : start + rows], chosen)
+    turned = (iota((256, 256), 0) + iota((256, 256), 1) == 144).astype(jnp.bfloat16)
+    return jnp.dot(chosen.astype(jnp.bfloat16), turned, preferred_element_type=jnp.float32)
+
+
+def lay_band(taps, base, moved, band, first, rows, total_rows, backward):
+    kernels, blocks = taps.shape[0], rows // 4
+    for b in range(kernels):
+        base[b] = base_rows(taps, b, first, rows, total_rows, backward)
+
+    def move(n, carry):
+        for a in range(4):
+            for b in range(kernels):
+                row = jnp.broadcast_to(base[b, pl.ds(n * 4 + a, 1)], (16, 256))
+                moved[a, n, b] = pltpu.roll(row, 0, 1, stride=1, stride_axis=0).astype(jnp.bfloat16)
+        return carry
+
+    lax.fori_loop(0, blocks, move, 0)
+    place = iota((256, 256), 1)
+    west, east = place - 128, place - 192
+    own = lax.div(place, 16) * 32 + 8 + lax.rem(place, 16)
+    side = jnp.where(place < 192, lax.div(west, 8) * 32 + lax.rem(west, 8), lax.div(east, 8) * 32 + 24 + lax.rem(east, 8))
+    wanted = jnp.where(place < 128, own, side)
+    for a in range(4):
+        table = (iota((256, 256), 0) == wanted - 32 * a).astype(jnp.bfloat16)
+
+        def place_rows(group, carry):
+            at = pl.ds(group * 4, 4)
+            rows_in = moved[a, at].reshape(4 * kernels * 16, 256)
+            out = jnp.dot(rows_in, table, preferred_element_type=jnp.float32).astype(jnp.bfloat16)
+            band[at, :, a] = out.reshape(4, kernels, 16, 256)
+            return carry
+
+        lax.fori_loop(0, blocks // 4, place_rows, 0)
+
+
+def gelu_slope(values):
+    cdf = 0.5 * (1.0 + lax.erf(values * math.sqrt(0.5)))
+    return cdf + values * (jnp.exp(values * values * -0.5) * (1.0 / math.sqrt(2.0 * math.pi)))
+
+
+def apply_blocks(band, halo, flat, part, channels, blocks):
+    def block(step, carry):
+        n = part * blocks + step
+        out = jnp.dot(band[n].reshape(192, 256), halo.window(n * 4), preferred_element_type=jnp.float32).astype(jnp.bfloat16)
+        at = pl.ds(pl.multiple_of(n * 64, 64), 64)
+        for b in range(3):
+            flat[at, b * channels : (b + 1) * channels] = out[b * 64 : (b + 1) * 64]
+        return carry
+
+    lax.fori_loop(0, blocks, block, 0)
+
+
+def block_kernel(
+    scale, features_hbm, filter_basis, half_widths, mixing_hbm, bias, cotangent_hbm, grad_hbm, mixing_out,
+    own, west_in, east_in, west_out, east_out, send, recv,
+    g_own, g_west_in, g_east_in, g_west_out, g_east_out, g_send, g_recv,
+    mixing, cotangent, result, flat, local, stage, taps, base, moved, band, g_band, load_sem, store_sem, *sum_refs):
+    rows, width, channels = cotangent.shape
+    kernels = filter_basis.shape[0]
+    total_rows = filter_basis.shape[3]
+    parts, part_rows = 5, rows // 5
+    blocks = part_rows // 4
+    pairs = part_rows // 2
+    loads = [
+        pltpu.make_async_copy(features_hbm, own.at[2 : rows + 2], load_sem.at[0]),
+        pltpu.make_async_copy(mixing_hbm, mixing, load_sem.at[1]),
+        pltpu.make_async_copy(cotangent_hbm, cotangent, load_sem.at[2]),
+    ]
+    for load in loads:
+        load.start()
+    greet(list(halo_peers().values()) + sum_peers())
+    cuts = [0] + [pairs * part + 1 for part in range(1, parts)] + [rows // 2]
+    halo = Halo(own, west_in, east_in, west_out, east_out, send, recv, cuts)
+    g_halo = Halo(g_own, g_west_in, g_east_in, g_west_out, g_east_out, g_send, g_recv, [pairs * part for part in range(parts + 1)])
+    loads[0].wait()
+    for part in range(parts):
+        lo, hi = cuts[part], cuts[part + 1]
+        halo.pack(lo, own[2 + 2 * lo : 2 + 2 * hi].astype(jnp.float32))
+        halo.send_part(part)
+        if part == 0:
+            halo.send_north()
+    halo.send_south()
+
+    first = pl.multiple_of(lax.axis_index("lat") * rows, 8)
+    lay_taps(filter_basis, half_widths, stage, taps)
+    lay_band(taps, base, moved, band, first, rows, total_rows, False)
+    lay_band(taps, base, moved, g_band, first, rows, total_rows, True)
+    loads[1].wait()
+    loads[2].wait()
+    halo.wait(halo.top)
+    cells = part_rows * width
+    for part in range(parts):
+        halo.wait(halo.parts[part])
+        if part == parts - 1:
+            halo.wait(halo.bottom)
+        apply_blocks(band, halo, flat, part, channels, blocks)
+        here = flat[part * cells : (part + 1) * cells]
+        pre = jnp.dot(here, mixing[...], preferred_element_type=jnp.float32) + bias[...]
+        at = part * part_rows
+        cot = cotangent[at : at + part_rows].reshape(cells, channels).astype(jnp.float32)
+        grad = cot * gelu_slope(pre)
+        grad_rows = grad.reshape(part_rows, width, channels)
+        grad = grad.astype(jnp.bfloat16)
+        g_own[2 + at : 2 + at + part_rows] = grad.reshape(part_rows, width, channels)
+        g_halo.pack(at // 2, grad_rows)
+        g_halo.send_part(part)
+        if part == 0:
+            g_halo.send_north()
+        if part == parts - 1:
+            g_halo.send_south()
+        outer = lax.dot_general(here, grad, (((0,), (0,)), ((), ())), preferred_element_type=jnp.float32)
+        outer = outer.reshape(local.shape)
+        if part == 0:
+            local[...] = outer
+        else:
+            local[...] += outer
+
+    work = SumOverAll(local, sum_refs, scale)
+    steps = [work.start_core, work.finish_core_start_x, work.finish_x_start_z, work.finish_z_start_y, work.finish_y_start_gather]
+    stores = []
+    g_halo.wait(g_halo.top)
+    g_halo.wait(g_halo.parts[0])
+    for part in range(parts):
+        steps[part]()
+        if part < parts - 1:
+            g_halo.wait(g_halo.parts[part + 1])
+        else:
+            g_halo.wait(g_halo.bottom)
+        apply_blocks(g_band, g_halo, flat, part, channels, blocks)
+        here = flat[part * cells : (part + 1) * cells]
+        at = part * part_rows
+        branch = cotangent[at : at + part_rows].reshape(cells, channels).astype(jnp.float32)
+        for b in range(kernels):
+            mix = mixing[b * channels : (b + 1) * channels]
+            branch = branch + lax.dot_general(
+                here[:, b * channels : (b + 1) * channels], mix, (((1,), (1,)), ((), ())), preferred_element_type=jnp.float32)
+        result[at : at + part_rows] = branch.astype(jnp.bfloat16).reshape(part_rows, width, channels)
+        stores.append(pltpu.make_async_copy(
+            result.at[at : at + part_rows], grad_hbm.at[at : at + part_rows], store_sem.at[part]))
+        stores[-1].start()
     work.finish_z_gather_x()
     work.finish_x_gather_core()
-    work.finish(out)
-
-
-def sum_over_all(local, scale):
-    rows, channels = local.shape
-    part_rows = rows // (2 * SIZE_X)
+    work.finish(mixing_out)
+    for store in stores:
+        store.wait()
+
+
+def halo_buffers(rows, channels, parts):
+    side = pltpu.VMEM((rows // 2 + 2, 16, channels), jnp.bfloat16)
+    out = pltpu.VMEM((rows // 2, 16, channels), jnp.bfloat16)
+    copies = 2 * parts + 6
+    return [
+        pltpu.VMEM((rows + 4, 16, channels), jnp.bfloat16), side, side, out, out,
+        pltpu.SemaphoreType.DMA((copies,)), pltpu.SemaphoreType.DMA((copies,)),
+    ]
+
+
+def per_device(features, filter_basis, half_widths, mixing, channel_bias, cotangent):
+    rows, width, channels = features.shape
+    kernels, taps_lat, taps_lon, total_rows = filter_basis.shape
+    cells = rows * width
+    cell_count = cells * lax.axis_size("lat") * lax.axis_size("lon")
+    sum_rows = kernels * channels // (2 * SIZE_X)
+    blocks = rows // 4
+    lanes = -(-total_rows // 128) * 128
+    anywhere, vmem = pl.BlockSpec(memory_space=pl.ANY), pl.BlockSpec(memory_space=pltpu.VMEM)
+    band = pltpu.VMEM((blocks, kernels, 4, 16, 256), jnp.bfloat16)
     return pl.pallas_call(
-        lambda *refs: sum_kernel(scale, *refs),
-        out_shape=jax.ShapeDtypeStruct((rows, channels), jnp.bfloat16),
-        in_specs=[pl.BlockSpec(memory_space=pltpu.VMEM)],
-        out_specs=pl.BlockSpec(memory_space=pltpu.VMEM),
-        scratch_shapes=sum_buffers(part_rows, channels),
+        lambda *refs: block_kernel(math.sqrt(cell_count), *refs),
+        out_shape=(
+            jax.ShapeDtypeStruct((rows, width, channels), jnp.bfloat16),
+            jax.ShapeDtypeStruct((kernels * channels, channels), jnp.bfloat16),
+        ),
+        in_specs=[anywhere, vmem, vmem, anywhere, vmem, anywhere],
+        out_specs=(anywhere, vmem),
+        scratch_shapes=[
+            *halo_buffers(rows, channels, 5),
+            *halo_buffers(rows, channels, 5),
+            pltpu.VMEM((kernels * channels, channels), jnp.bfloat16),
+            pltpu.VMEM((rows, width, channels), jnp.bfloat16),
+            pltpu.VMEM((rows, width, channels), jnp.bfloat16),
+            pltpu.VMEM((cells, kernels * channels), jnp.bfloat16),
+            pltpu.VMEM((2, SIZE_X, sum_rows, channels), jnp.float32),
+            pltpu.VMEM((256, lanes), jnp.float32),
+            pltpu.VMEM((kernels, lanes + 16, 256), jnp.float32),
+            pltpu.VMEM((kernels, rows, 256), jnp.float32),
+            pltpu.VMEM((4, blocks, kernels, 16, 256), jnp.bfloat16),
+            band,
+            band,
+            pltpu.SemaphoreType.DMA((3,)),
+            pltpu.SemaphoreType.DMA((5,)),
+            *sum_buffers(sum_rows, channels),
+        ],
         compiler_params=pltpu.CompilerParams(
-            collective_id=0, has_side_effects=True, vmem_limit_bytes=32 * 1024 * 1024),
-    )(local.reshape(2, SIZE_X, part_rows, channels))
-
-
-def extended_2(block, sides, width, periodic):
-    for axis, dim in sides:
-        count = lax.axis_size(axis)
-        forward = [(i, i + 1) for i in range(count - 1)]
-        if periodic:
-            forward.append((count - 1, 0))
-        backward = [(target, source) for source, target in forward]
-        low = lax.ppermute(
-            lax.slice_in_dim(block, block.shape[dim] - width, None, axis=dim), axis, forward
-        )
-        high = lax.ppermute(lax.slice_in_dim(block, 0, width, axis=dim), axis, backward)
-        block = jnp.concatenate([low, block, high], axis=dim)
-    return block
-
-
-def gelu_exact(values):
-    return jax.nn.gelu(values, approximate=False)
-
-
-def basis_window(filter_basis, half_widths, row_start, rows_here, reach, halo):
-    taps_lon = 2 * halo + 1
-    offsets = jnp.abs(jnp.arange(taps_lon, dtype=jnp.int32) - halo)
-    allowed = (offsets[:, None] <= half_widths[None, :]).astype(jnp.float32)
-    masked = filter_basis.astype(jnp.float32) * allowed[None, None]
-    padded = jnp.pad(masked, ((0, 0), (0, 0), (0, 0), (reach, reach)))
-    return lax.dynamic_slice_in_dim(padded, row_start, rows_here + 2 * reach, 3)
-
-
-def band_matrix(rows_taps, shift_table):
-    band = jnp.einsum("bsqa,qvu->avbsu", rows_taps, shift_table, precision=lax.Precision.HIGHEST)
-    count_rows, width_out, kernels, taps_lat, width_in = band.shape
-    return band.reshape(count_rows, width_out * kernels, taps_lat * width_in).astype(jnp.bfloat16)
-
-
-def stacked_rows(extended, rows_here, taps_lat):
-    pieces = [extended[offset : offset + rows_here] for offset in range(taps_lat)]
-    stacked = jnp.stack(pieces, axis=1)
-    return stacked.reshape(rows_here, -1, stacked.shape[-1])
-
-
-def contract(band, windows):
-    return jnp.einsum("anm,amc->anc", band, windows, preferred_element_type=jnp.float32)
-
-
-def extend_lat(block, reach):
-    return extended_2(block, (("lat", 0),), reach, False)
-
-
-def apply_band(band, lat_ext, halo, rows_here, taps_lat):
-    padded = extended_2(lat_ext, (("lon", 1),), halo, True)
-    return contract(band, stacked_rows(padded, rows_here, taps_lat))
-
-
-def per_device(features, filter_basis, half_widths, mixing, channel_bias, cotangent):
-    rows_here, width_here, channels = features.shape
-    kernels, taps_lat, taps_lon, total_rows = filter_basis.shape
-    reach = (taps_lat - 1) // 2
-    halo = (taps_lon - 1) // 2
-    row_start = lax.axis_index("lat") * rows_here
-    window = basis_window(filter_basis, half_widths, row_start, rows_here, reach, halo)
-    span = width_here + 2 * halo
-    tap_ids = jnp.arange(taps_lon, dtype=jnp.int32)[:, None, None]
-    out_ids = jnp.arange(width_here, dtype=jnp.int32)[None, :, None]
-    in_ids = jnp.arange(span, dtype=jnp.int32)[None, None, :]
-    forward_table = (in_ids - out_ids == tap_ids).astype(jnp.float32)
-    backward_table = (out_ids + 2 * halo - in_ids == tap_ids).astype(jnp.float32)
-    forward_band = band_matrix(window[:, :, :, reach : reach + rows_here], forward_table)
-    backward_rows = jnp.stack(
-        [
-            window[:, taps_lat - 1 - offset, :, offset : offset + rows_here]
-            for offset in range(taps_lat)
-        ],
-        axis=1,
-    )
-    backward_band = band_matrix(backward_rows, backward_table)
-    filtered = apply_band(forward_band, extend_lat(features, reach), halo, rows_here, taps_lat)
-    flat = filtered.astype(jnp.bfloat16).reshape(rows_here * width_here, kernels * channels)
-    pre = jnp.dot(flat, mixing, preferred_element_type=jnp.float32) + channel_bias
-    cell_grads = cotangent.reshape(rows_here * width_here, channels).astype(jnp.float32)
-    _, pullback = jax.vjp(gelu_exact, pre)
-    (grad_pre,) = pullback(cell_grads)
-    grad_pre = grad_pre.astype(jnp.bfloat16)
-    local_sum = lax.dot_general(
-        flat, grad_pre, (((0,), (0,)), ((), ())), preferred_element_type=jnp.float32
-    )
-    cell_count = rows_here * lax.axis_size("lat") * width_here * lax.axis_size("lon")
-    mixing_grad = sum_over_all(local_sum, math.sqrt(cell_count))
-    grad_grid = grad_pre.reshape(rows_here, width_here, channels)
-    spread = apply_band(backward_band, extend_lat(grad_grid, reach), halo, rows_here, taps_lat)
-    transposed = (
-        mixing.reshape(kernels, channels, channels)
-        .transpose(0, 2, 1)
-        .reshape(kernels * channels, channels)
-    )
-    branch = jnp.dot(
-        spread.astype(jnp.bfloat16).reshape(rows_here * width_here, kernels * channels),
-        transposed,
-        preferred_element_type=jnp.float32,
-    )
-    input_grad = (cell_grads + branch).astype(jnp.bfloat16).reshape(rows_here, width_here, channels)
-    return (input_grad, mixing_grad)
+            collective_id=0, has_side_effects=True, vmem_limit_bytes=48 * 1024 * 1024),
+    )(features, filter_basis, half_widths.reshape(1, total_rows), mixing, channel_bias.reshape(1, channels), cotangent)
 
 
 def solution(mesh):

time: 196 us -> 89.3 us (0.46)
  local copies, waits for them, and re-layouts: 63.6 us -> 7.1 us
  Pallas kernels: 38.8 us -> 81.3 us
  starting transfers between devices: 40.5 us -> 0 us
  matrix products: 35.8 us -> 0 us
  waiting for transfers between devices: 12 us -> 0 us
  other arithmetic: 3.63 us -> 0 us
    pallas_call x1, Pallas kernels: 38.8 us -> 81.3 us  [per_device(): pl.pallas_call(lambda *refs: block_kernel(math.sqrt(cell_count), *refs),...]
    ppermute x8 -> x0, starting transfers between devices: 40.5 us -> none  [the longest x4 25.6 us: extended_2(): lax.ppermute(lax.slice_in_dim(block, 0, width, axis=dim), axis, backward)]
    dot_general x7 -> x0, matrix products: 35.8 us -> none  [the longest x2 13.5 us: contract(): jnp.einsum('anm,amc->anc', band, windows, preferred_element_type=jnp.floa...]
    another operation x5 -> x0, local copies, waits for them, and re-layouts: 20.8 us -> none  [the longest x4 20.1 us: stacked_rows(): stacked = jnp.stack(pieces, axis=1)]
    ppermute x8 -> x0, waiting for transfers between devices: 12 us -> none  [the longest x4 6.24 us: extended_2(): lax.ppermute(lax.slice_in_dim(block, block.shape[dim] - width, None, axis...]
    unnamed x29 -> x11, local copies, waits for them, and re-layouts: 15.9 us -> 6.41 us
    reshape x2, local copies, waits for them, and re-layouts: 9.15 us -> 0.69 us  [the longest x1 0.69 us: per_device(): half_widths.reshape(1, total_rows)]
    convert_element_type x2 -> x0, local copies, waits for them, and re-layouts: 7.72 us -> none  [band_matrix(): band.reshape(count_rows, width_out * kernels, taps_lat * width_in)]
  transfers between devices with their start and end apart: 8 -> 0, of which waited for: 3 -> 0; matrix products, arithmetic and copies ran while one was open for 16% -> 0% of each run, Pallas kernels for 20% -> 0%
where the time goes in v2:
time: 89.3 us; the launch traced here: 89 us
  Pallas kernels  81.3 us (91%)
  local copies, waits for them, and re-layouts  7.1 us (8%)
    pallas_call x1, Pallas kernels, per_device(): pl.pallas_call(lambda *refs: block_kernel(math.sqrt(cell_count), *refs),...  81.3 us
    unnamed x11, local copies, waits for them, and re-layouts  6.41 us

profile of v2, /device:TPU:1, one launch (start us, length us, event | category | flops | bytes accessed | tf_op | source)
XLA Modules:
  0.0 89.0 jit_solution(13106663548782453215)
XLA Ops:
  0.6 0.0 copy-start.3
  0.6 0.7 reshape.10.refs_2_
  1.3 0.0 copy-done.3
  1.3 1.0 %copy.8.refs_1_ = bf16[3,5,17,320]{3,2,1,0:T(8,128)(2,1)S(1)} copy(bf16[3,5,17,320]{3,0,2,1:T(4,128)(2,1)} %param.7) | data formatting | bytes 326400 | tf_op args[1]
  2.3 0.0 copy-start
  2.3 1.2 %copy-done = bf16[80,16,384]{2,1,0:T(8,128)(2,1)S(1)} copy-done((bf16[80,16,384]{2,1,0:T(8,128)(2,1)S(1)}, bf16[80,16,384]{2,1,0:T(8,128)(2,1)}, u32[]{:S(2)}) %copy-start) | copy-done | bytes 983064
  3.5 0.0 copy-start.1
  3.5 1.2 %copy-done.1 = bf16[80,16,384]{2,1,0:T(8,128)(2,1)S(1)} copy-done((bf16[80,16,384]{2,1,0:T(8,128)(2,1)S(1)}, bf16[80,16,384]{2,1,0:T(8,128)(2,1)}, u32[]{:S(2)}) %copy-start.1) | copy-done | bytes 983064
  4.7 0.0 copy-start.2
  4.7 1.2 %copy-done.2 = bf16[1152,384]{1,0:T(8,128)(2,1)S(1)} copy-done((bf16[1152,384]{1,0:T(8,128)(2,1)S(1)}, bf16[1152,384]{1,0:T(8,128)(2,1)}, u32[]{:S(2)}) %copy-start.2) | copy-done | bytes 884760
  5.9 81.3 %shard_map.77 = (bf16[80,16,384]{2,1,0:T(8,128)(2,1)S(1)}, bf16[1152,384]{1,0:T(8,128)(2,1)S(1)}) custom-call(bf16[80,16,384]{2,1,0:T(8,128)(2,1)S(1)} %copy-done, bf16[3,5,17,320]{3,2,1,0:T(8,128)(2,1)S(1)} %copy.8.refs_1_, s32[1,320]{1,0:T(1,128)S(1)} %reshape.10.refs_2_, bf16[1152,384]{1,0:T(8,128)(2,1)S(1)} %copy-done.2, f32[1,384]{1,0:T(1,128)S(1)} %reshape.11.refs_4_, ...), custom_call_target="tpu_custom_call" | custom-call | tf_op jit(solution)/shard_map/pallas_call | solution.py:435
  87.2 0.9 %copy.11 = bf16[80,16,384]{2,1,0:T(8,128)(2,1)} copy(bf16[80,16,384]{2,1,0:T(8,128)(2,1)S(1)} %get-tuple-element.4) | data formatting | bytes 1966080
  88.1 0.9 %copy.12 = bf16[1152,384]{1,0:T(8,128)(2,1)} copy(bf16[1152,384]{1,0:T(8,128)(2,1)S(1)} %get-tuple-element.5) | data formatting | bytes 1769472
  (1 shorter events, 0.0 us)
Async XLA Ops:
  0.6 0.7 copy-start.3
  2.3 1.2 %copy-start = (bf16[80,16,384]{2,1,0:T(8,128)(2,1)S(1)}, bf16[80,16,384]{2,1,0:T(8,128)(2,1)}, u32[]{:S(2)}) copy-start(bf16[80,16,384]{2,1,0:T(8,128)(2,1)} %refs_0_.1) | copy-start | bytes 2949124
  3.5 1.2 %copy-start.1 = (bf16[80,16,384]{2,1,0:T(8,128)(2,1)S(1)}, bf16[80,16,384]{2,1,0:T(8,128)(2,1)}, u32[]{:S(2)}) copy-start(bf16[80,16,384]{2,1,0:T(8,128)(2,1)} %refs_5_.1) | copy-start | bytes 2949124
  4.7 1.2 %copy-start.2 = (bf16[1152,384]{1,0:T(8,128)(2,1)S(1)}, bf16[1152,384]{1,0:T(8,128)(2,1)}, u32[]{:S(2)}) copy-start(bf16[1152,384]{1,0:T(8,128)(2,1)} %refs_3_.1) | copy-start | bytes 2654212

commit v3 on v2

v3 whole, which is shorter than its diff:
```python
import math

import jax
import jax.numpy as jnp
from jax import lax
from jax.experimental import pallas as pl
from jax.experimental.pallas import tpu as pltpu
from jax.sharding import PartitionSpec as P

MESH = pl.DeviceIdType.MESH
SIZE_X_LO, SIZE_Z, SIZE_Y = 2, 8, 8
SIZE_X = 4


def position():
    lon, lat = lax.axis_index("lon"), lax.axis_index("lat")
    x = lax.div(lat, 2) * SIZE_X_LO + lax.div(lon, SIZE_Z * SIZE_Y)
    z = lax.rem(lax.div(lon, SIZE_Y), SIZE_Z)
    return x, z, lax.rem(lon, SIZE_Y), lax.rem(lat, 2)


def device(x, z, y, core):
    lon = (lax.rem(x, SIZE_X_LO) * SIZE_Z + z) * SIZE_Y + y
    return {"lon": lon, "lat": lax.div(x, SIZE_X_LO) * 2 + core}


def sum_peers():
    x, z, y, core = position()
    peers = [device(x, z, y, 1 - core)]
    peers += [device(lax.rem(x + d, SIZE_X), z, y, core) for d in range(1, SIZE_X)]
    peers += [device(x, lax.rem(z + d, SIZE_Z), y, core) for d in range(1, SIZE_Z)]
    peers += [device(x, z, lax.rem(y + d, SIZE_Y), core) for d in range(1, SIZE_Y)]
    return peers


def greet(peers):
    barrier = pltpu.get_barrier_semaphore()
    for peer in peers:
        pl.semaphore_signal(barrier, inc=1, device_id=peer, device_id_type=MESH)


def await_greetings(count):
    pl.semaphore_wait(pltpu.get_barrier_semaphore(), count)


SHARE = 4
Y_ORDER = (4, 3, 5, 2, 6, 1, 7, 0)
GATHER_ORDER = (0, 1, 7, 2, 6, 3, 5, 4)


def tile_count(part_rows, channels):
    tiles = (part_rows // 16) * (channels // 128)
    assert (SIZE_Y - 1) * SHARE <= tiles + 1 <= SIZE_Y * SHARE
    return tiles


def sum_buffers():
    pieces = (SIZE_Y, SIZE_X, SHARE, 16, 128)
    copies = SIZE_Y + 2 * SIZE_Y * (SIZE_X - 1) + 2 * (SIZE_Y - 1) + SIZE_Z - 1 + SIZE_X
    return [
        pltpu.VMEM((2, *pieces), jnp.float32),
        pltpu.VMEM(pieces, jnp.float32),
        pltpu.VMEM(pieces, jnp.bfloat16),
        pltpu.VMEM((SIZE_X - 1, SIZE_Y, SHARE, 16, 128), jnp.bfloat16),
        pltpu.VMEM((SIZE_Y - 1, SHARE, 16, 128), jnp.bfloat16),
        pltpu.VMEM((SIZE_Y - 1, SHARE, 16, 128), jnp.bfloat16),
        pltpu.VMEM((SIZE_Z, SHARE, 16, 128), jnp.bfloat16),
        pltpu.VMEM((2, SIZE_X, SIZE_Y, SHARE, 16, 128), jnp.bfloat16),
        pltpu.SemaphoreType.DMA((copies,)),
        pltpu.SemaphoreType.DMA((copies,)),
    ]


class SumOverAll:
    def __init__(self, rows, channels, buffers, scale):
        (self.local, self.half, self.x_out, self.x_in, self.y_out, self.y_in, self.z_all, self.done, self.send, self.recv) = buffers
        self.rows, self.lanes, self.tiles, self.scale = rows, channels // 128, tile_count(rows, channels), scale
        self.x, self.z, self.y, self.core = position()
        self.used, self.sent = 0, []

    def copy(self, src, dst, peer):
        index = self.used
        self.used += 1
        copy = pltpu.make_async_remote_copy(
            src_ref=src, dst_ref=dst, send_sem=self.send.at[index], recv_sem=self.recv.at[index],
            device_id=peer, device_id_type=MESH)
        copy.start()
        self.sent.append(copy)
        return copy

    def other_core(self):
        return device(self.x, self.z, self.y, 1 - self.core)

    def other_x(self, d):
        return device(lax.rem(self.x + d, SIZE_X), self.z, self.y, self.core)

    def other_y(self, d):
        return device(self.x, self.z, lax.rem(self.y + d, SIZE_Y), self.core)

    def other_z(self, d):
        return device(self.x, lax.rem(self.z + d, SIZE_Z), self.y, self.core)

    def places(self, core, part):
        for t in range(self.tiles):
            row = (core * SIZE_X + part) * self.rows + t // self.lanes * 16
            lane = t % self.lanes * 128
            yield t // SHARE, t % SHARE, slice(row, row + 16), slice(lane, lane + 128)

    def clear(self):
        self.local[:, SIZE_Y - 2 :] = jnp.zeros_like(self.local[:, SIZE_Y - 2 :])

    def lay(self, values, more):
        for core in range(2):
            for part in range(SIZE_X):
                for y, slot, rows, lanes in self.places(core, part):
                    self.local[core, y, part, slot] = values[rows, lanes] + more[rows, lanes]

    def start_core(self):
        self.from_core = {}
        for d in Y_ORDER:
            y = lax.rem(self.y + d, SIZE_Y)
            self.from_core[d] = self.copy(self.local.at[1 - self.core, y], self.half.at[y], self.other_core())

    def core_to_x(self):
        self.from_x = {}
        for d in Y_ORDER:
            y = lax.rem(self.y + d, SIZE_Y)
            self.from_core[d].wait_recv()
            total = self.half[y] + self.local[self.core, y]
            self.half[y] = total
            self.x_out[y] = total.astype(jnp.bfloat16)
            self.from_x[d] = [
                self.copy(self.x_out.at[y, lax.rem(self.x + e, SIZE_X)], self.x_in.at[e - 1, y], self.other_x(e))
                for e in (2, 1, 3)
            ]

    def x_to_y(self):
        self.from_y = []
        for d in Y_ORDER:
            y = lax.rem(self.y + d, SIZE_Y)
            total = self.half[y, self.x]
            for copy in self.from_x[d]:
                copy.wait_recv()
            for e in range(SIZE_X - 1):
                total = total + self.x_in[e, y].astype(jnp.float32)
            if d:
                self.y_out[d - 1] = total.astype(jnp.bfloat16)
                self.from_y.append(self.copy(self.y_out.at[d - 1], self.y_in.at[d - 1], self.other_y(d)))
            else:
                self.half[y, self.x] = total

    def y_to_z(self):
        total = self.half[self.y, self.x]
        for copy in self.from_y:
            copy.wait_recv()
        for d in range(SIZE_Y - 1):
            total = total + self.y_in[d].astype(jnp.float32)
        self.z_all[self.z] = total.astype(jnp.bfloat16)
        piece = self.z_all.at[self.z]
        self.from_z = [self.copy(piece, piece, self.other_z(d)) for d in (4, 3, 5, 2, 6, 1, 7)]

    def spread_x(self, d):
        y = lax.rem(self.y + SIZE_Y - d, SIZE_Y)
        piece = self.done.at[self.core, self.x, y]
        for e in (2, 1, 3):
            self.gathered[e].append(self.copy(piece, piece, self.other_x(e)))

    def z_to_gather(self):
        for copy in self.from_z:
            copy.wait_recv()
        total = self.z_all[0].astype(jnp.float32)
        for other in range(1, SIZE_Z):
            total = total + self.z_all[other].astype(jnp.float32)
        self.done[self.core, self.x, self.y] = (total / self.scale).astype(jnp.bfloat16)
        piece = self.done.at[self.core, self.x, self.y]
        self.y_gathered = {d: self.copy(piece, piece, self.other_y(d)) for d in (4, 3, 5, 2, 6, 1, 7)}
        self.gathered = {e: [] for e in range(1, SIZE_X)}
        self.spread_x(0)

    def gather_y(self):
        for d in GATHER_ORDER[1:]:
            self.y_gathered[d].wait_recv()
            self.spread_x(d)
        self.spread_core(0)

    def spread_core(self, e):
        part = self.done.at[self.core, lax.rem(self.x + SIZE_X - e, SIZE_X)]
        self.copy(part, part, self.other_core())

    def gather_x(self):
        for e in (1, 3, 2):
            for copy in self.gathered[e]:
                copy.wait_recv()
            self.spread_core(e)

    def finish(self, out):
        for copy in self.sent[-SIZE_X:]:
            copy.wait_recv()
        for core in range(2):
            for part in range(SIZE_X):
                for y, slot, rows, lanes in self.places(core, part):
                    out[rows, lanes] = self.done[core, part, y, slot]
        for copy in self.sent:
            copy.wait_send()


def halo_peers():
    lon, lat = lax.axis_index("lon"), lax.axis_index("lat")
    count_lon, count_lat = lax.axis_size("lon"), lax.axis_size("lat")
    east, west = lax.rem(lon + 1, count_lon), lax.rem(lon + count_lon - 1, count_lon)
    south, north = lax.rem(lat + 1, count_lat), lax.rem(lat + count_lat - 1, count_lat)
    return {
        (row, column): {"lon": at_lon, "lat": at_lat}
        for row, at_lat in ((-1, north), (0, lat), (1, south))
        for column, at_lon in ((-1, west), (0, lon), (1, east))
        if (row, column) != (0, 0)
    }


class Halo:
    def __init__(self, own, west_in, east_in, west_out, east_out, send, recv, cuts):
        self.own, self.west_in, self.east_in = own, west_in, east_in
        self.west_out, self.east_out, self.send, self.recv = west_out, east_out, send, recv
        self.peers, self.rows, self.cuts, self.used = halo_peers(), own.shape[0] - 4, cuts, 0
        self.pairs, self.parts, self.top, self.bottom = self.rows // 2, [], [], []

    def copy(self, src, dst, peer):
        index = self.used
        self.used += 1
        copy = pltpu.make_async_remote_copy(
            src_ref=src, dst_ref=dst, send_sem=self.send.at[index], recv_sem=self.recv.at[index],
            device_id=self.peers[peer], device_id_type=MESH)
        copy.start()
        return copy

    def pack(self, first, values):
        pairs, channels = values.shape[0] // 2, values.shape[-1]
        split = values.reshape(pairs, 2, 16, channels)
        self.west_out[first : first + pairs] = split[:, :, :8].reshape(pairs, 16, channels).astype(jnp.bfloat16)
        self.east_out[first : first + pairs] = split[:, :, 8:].reshape(pairs, 16, channels).astype(jnp.bfloat16)

    def send_part(self, part):
        lo, hi = self.cuts[part], self.cuts[part + 1]
        self.parts.append([
            self.copy(self.east_out.at[lo:hi], self.west_in.at[lo + 1 : hi + 1], (0, 1)),
            self.copy(self.west_out.at[lo:hi], self.east_in.at[lo + 1 : hi + 1], (0, -1)),
        ])

    def send_north(self):
        rows, last = self.rows, self.pairs + 1
        self.bottom = [
            self.copy(self.own.at[2:4], self.own.at[rows + 2 : rows + 4], (-1, 0)),
            self.copy(self.east_out.at[0:1], self.west_in.at[last : last + 1], (-1, 1)),
            self.copy(self.west_out.at[0:1], self.east_in.at[last : last + 1], (-1, -1)),
        ]

    def send_south(self):
        rows, last = self.rows, self.pairs - 1
        self.top = [
            self.copy(self.own.at[rows : rows + 2], self.own.at[0:2], (1, 0)),
            self.copy(self.east_out.at[last : last + 1], self.west_in.at[0:1], (1, 1)),
            self.copy(self.west_out.at[last : last + 1], self.east_in.at[0:1], (1, -1)),
        ]

    def wait(self, copies):
        for copy in copies:
            copy.wait()

    def window(self, first):
        channels = self.own.shape[-1]
        pair = first // 2
        return jnp.concatenate([
            self.own[first : first + 8].reshape(128, channels),
            self.west_in[pair : pair + 4].reshape(64, channels),
            self.east_in[pair : pair + 4].reshape(64, channels),
        ], axis=0)


def iota(shape, dim):
    return lax.broadcasted_iota(jnp.int32, shape, dim)


def lay_taps(filter_basis, half_widths, stage, taps):
    taps_lat, taps_lon, kernels, rows = filter_basis.shape
    allowed = jnp.abs(iota((taps_lon, rows), 0) - taps_lon // 2) <= half_widths[...].reshape(1, rows)
    stage[...] = jnp.zeros_like(stage)
    taps[...] = jnp.zeros_like(taps)
    for b in range(kernels):
        for s in range(taps_lat):
            values = jnp.where(allowed, filter_basis[s].astype(jnp.float32)[:, b], 0.0)
            stage[s * 32 : s * 32 + taps_lon, 0:rows] = values
        taps[b, 8 : 8 + stage.shape[1]] = stage[...].T


def base_rows(taps, b, first, rows, total_rows, backward):
    reach = 2
    near = taps[b, pl.ds(first, rows + 16)]
    lane = iota((rows, 256), 1)
    if not backward:
        source = iota((rows, 256), 0) + first + lax.div(lane, 32) - reach
        return jnp.where((source >= 0) & (source < total_rows), near[8 : 8 + rows], 0.0)
    chosen = jnp.zeros((rows, 256), jnp.float32)
    for s in range(5):
        start = 8 + reach - s
        chosen = jnp.where(lax.div(lane, 32) == s, near[start : start + rows], chosen)
    turned = (iota((256, 256), 0) + iota((256, 256), 1) == 144).astype(jnp.bfloat16)
    return jnp.dot(chosen.astype(jnp.bfloat16), turned, preferred_element_type=jnp.float32)


def lay_band(taps, base, moved, band, first, rows, total_rows, backward):
    kernels, blocks = taps.shape[0], rows // 4
    for b in range(kernels):
        base[b] = base_rows(taps, b, first, rows, total_rows, backward)

    def move(n, carry):
        for a in range(4):
            for b in range(kernels):
                row = jnp.broadcast_to(base[b, pl.ds(n * 4 + a, 1)], (16, 256))
                moved[a, n, b] = pltpu.roll(row, 0, 1, stride=1, stride_axis=0).astype(jnp.bfloat16)
        return carry

    lax.fori_loop(0, blocks, move, 0)
    place = iota((256, 256), 1)
    west, east = place - 128, place - 192
    own = lax.div(place, 16) * 32 + 8 + lax.rem(place, 16)
    side = jnp.where(place < 192, lax.div(west, 8) * 32 + lax.rem(west, 8), lax.div(east, 8) * 32 + 24 + lax.rem(east, 8))
    wanted = jnp.where(place < 128, own, side)
    for a in range(4):
        table = (iota((256, 256), 0) == wanted - 32 * a).astype(jnp.bfloat16)

        rows_in = moved[a].reshape(blocks * kernels * 16, 256)
        out = jnp.dot(rows_in, table, preferred_element_type=jnp.float32).astype(jnp.bfloat16)
        band[:, :, a] = out.reshape(blocks, kernels, 16, 256)


def gelu_slope(values):
    cdf = 0.5 * (1.0 + lax.erf(values * math.sqrt(0.5)))
    return cdf + values * (jnp.exp(values * values * -0.5) * (1.0 / math.sqrt(2.0 * math.pi)))


def apply_blocks(band, halo, flat, part, channels, blocks):
    for n in range(part * blocks, (part + 1) * blocks):
        out = jnp.dot(band[n].reshape(192, 256), halo.window(n * 4), preferred_element_type=jnp.float32).astype(jnp.bfloat16)
        for b in range(3):
            flat[n * 64 : (n + 1) * 64, b * channels : (b + 1) * channels] = out[b * 64 : (b + 1) * 64]


def block_kernel(
    scale, features_hbm, filter_hbm, half_widths, mixing_hbm, bias, cotangent_hbm, grad_hbm, mixing_out,
    own, west_in, east_in, west_out, east_out, send, recv,
    g_own, g_west_in, g_east_in, g_west_out, g_east_out, g_send, g_recv,
    mixing, cotangent, result, flat, local, stage, taps, base, moved, band, g_band, filter_basis, load_sem, store_sem, *sum_refs):
    rows, width, channels = cotangent.shape
    kernels, total_rows = filter_basis.shape[2:]
    parts, part_rows = 5, rows // 5
    blocks = part_rows // 4
    pairs = part_rows // 2
    loads = [
        pltpu.make_async_copy(features_hbm, own.at[2 : rows + 2], load_sem.at[0]),
        pltpu.make_async_copy(filter_hbm, filter_basis, load_sem.at[3]),
        pltpu.make_async_copy(mixing_hbm, mixing, load_sem.at[1]),
        pltpu.make_async_copy(cotangent_hbm, cotangent, load_sem.at[2]),
    ]
    for load in loads:
        load.start()
    peers = list(halo_peers().values()) + sum_peers()
    greet(peers)
    work = SumOverAll(mixing.shape[0] // (2 * SIZE_X), channels, sum_refs, scale)
    cuts = [0] + [pairs * part + 1 for part in range(1, parts)] + [rows // 2]
    halo = Halo(own, west_in, east_in, west_out, east_out, send, recv, cuts)
    g_halo = Halo(g_own, g_west_in, g_east_in, g_west_out, g_east_out, g_send, g_recv, [pairs * part for part in range(parts + 1)])
    loads[0].wait()
    for part in range(parts):
        lo, hi = cuts[part], cuts[part + 1]
        halo.pack(lo, own[2 + 2 * lo : 2 + 2 * hi].astype(jnp.float32))
    work.clear()
    await_greetings(len(peers))
    halo.send_north()
    for part in range(parts):
        halo.send_part(part)
    halo.send_south()

    first = pl.multiple_of(lax.axis_index("lat") * rows, 8)
    loads[1].wait()
    lay_taps(filter_basis, half_widths, stage, taps)
    lay_band(taps, base, moved, band, first, rows, total_rows, False)
    loads[2].wait()
    loads[3].wait()
    halo.wait(halo.top)
    cells = part_rows * width
    for part in range(parts):
        halo.wait(halo.parts[part])
        if part == parts - 1:
            halo.wait(halo.bottom)
        apply_blocks(band, halo, flat, part, channels, blocks)
        here = flat[part * cells : (part + 1) * cells]
        pre = jnp.dot(here, mixing[...], preferred_element_type=jnp.float32) + bias[...].reshape(1, channels)
        at = part * part_rows
        cot = cotangent[at : at + part_rows].reshape(cells, channels).astype(jnp.float32)
        grad = cot * gelu_slope(pre)
        grad_rows = grad.reshape(part_rows, width, channels)
        grad = grad.astype(jnp.bfloat16)
        g_own[2 + at : 2 + at + part_rows] = grad.reshape(part_rows, width, channels)
        g_halo.pack(at // 2, grad_rows)
        g_halo.send_part(part)
        if part == 0:
            g_halo.send_north()
        if part == parts - 1:
            g_halo.send_south()
        outer = lax.dot_general(here, grad, (((0,), (0,)), ((), ())), preferred_element_type=jnp.float32)
        if part == 0:
            local[...] = outer
        elif part < parts - 1:
            local[...] += outer
        else:
            work.lay(outer, local)

    work.start_core()
    work.core_to_x()
    lay_band(taps, base, moved, g_band, first, rows, total_rows, True)
    work.x_to_y()
    steps = {1: work.y_to_z, 3: work.z_to_gather, 4: work.gather_y}
    stores = []
    g_halo.wait(g_halo.top)
    g_halo.wait(g_halo.parts[0])
    for part in range(parts):
        if part in steps:
            steps[part]()
        if part < parts - 1:
            g_halo.wait(g_halo.parts[part + 1])
        else:
            g_halo.wait(g_halo.bottom)
        apply_blocks(g_band, g_halo, flat, part, channels, blocks)
        here = flat[part * cells : (part + 1) * cells]
        at = part * part_rows
        branch = cotangent[at : at + part_rows].reshape(cells, channels).astype(jnp.float32)
        for b in range(kernels):
            mix = mixing[b * channels : (b + 1) * channels]
            branch = branch + lax.dot_general(
                here[:, b * channels : (b + 1) * channels], mix, (((1,), (1,)), ((), ())), preferred_element_type=jnp.float32)
        result[at : at + part_rows] = branch.astype(jnp.bfloat16).reshape(part_rows, width, channels)
        stores.append(pltpu.make_async_copy(
            result.at[at : at + part_rows], grad_hbm.at[at : at + part_rows], store_sem.at[part]))
        stores[-1].start()
    work.gather_x()
    work.finish(mixing_out)
    for store in stores:
        store.wait()


def halo_buffers(rows, channels, parts):
    side = pltpu.VMEM((rows // 2 + 2, 16, channels), jnp.bfloat16)
    out = pltpu.VMEM((rows // 2, 16, channels), jnp.bfloat16)
    copies = 2 * parts + 6
    return [
        pltpu.VMEM((rows + 4, 16, channels), jnp.bfloat16), side, side, out, out,
        pltpu.SemaphoreType.DMA((copies,)), pltpu.SemaphoreType.DMA((copies,)),
    ]


def per_device(features, filter_basis, half_widths, mixing, channel_bias, cotangent):
    rows, width, channels = features.shape
    kernels, taps_lat, taps_lon, total_rows = filter_basis.shape
    cells = rows * width
    cell_count = cells * lax.axis_size("lat") * lax.axis_size("lon")
    blocks = rows // 4
    lanes = -(-total_rows // 128) * 128
    anywhere, vmem = pl.BlockSpec(memory_space=pltpu.HBM), pl.BlockSpec(memory_space=pltpu.VMEM)
    band = pltpu.VMEM((blocks, kernels, 4, 16, 256), jnp.bfloat16)
    return pl.pallas_call(
        lambda *refs: block_kernel(math.sqrt(cell_count), *refs),
        out_shape=(
            jax.ShapeDtypeStruct((rows, width, channels), jnp.bfloat16),
            jax.ShapeDtypeStruct((kernels * channels, channels), jnp.bfloat16),
        ),
        in_specs=[anywhere, anywhere, vmem, anywhere, vmem, anywhere],
        out_specs=(anywhere, vmem),
        scratch_shapes=[
            *halo_buffers(rows, channels, 5),
            *halo_buffers(rows, channels, 5),
            pltpu.VMEM((kernels * channels, channels), jnp.bfloat16),
            pltpu.VMEM((rows, width, channels), jnp.bfloat16),
            pltpu.VMEM((rows, width, channels), jnp.bfloat16),
            pltpu.VMEM((cells, kernels * channels), jnp.bfloat16),
            pltpu.VMEM((kernels * channels, channels), jnp.float32),
            pltpu.VMEM((256, lanes), jnp.float32),
            pltpu.VMEM((kernels, lanes + 16, 256), jnp.float32),
            pltpu.VMEM((kernels, rows, 256), jnp.float32),
            pltpu.VMEM((4, blocks, kernels, 16, 256), jnp.bfloat16),
            band,
            band,
            pltpu.VMEM((taps_lat, taps_lon, kernels, total_rows), jnp.bfloat16),
            pltpu.SemaphoreType.DMA((4,)),
            pltpu.SemaphoreType.DMA((5,)),
            *sum_buffers(),
        ],
        compiler_params=pltpu.CompilerParams(
            collective_id=0, has_side_effects=True, vmem_limit_bytes=56 * 1024 * 1024),
    )(features, filter_basis.transpose(1, 2, 0, 3), half_widths, mixing, channel_bias, cotangent)


def solution(mesh):
    return jax.shard_map(
        per_device,
        mesh=mesh,
        in_specs=(P("lat", "lon", None), P(), P(), P(), P(), P("lat", "lon", None)),
        out_specs=(P("lat", "lon", None), P()),
        check_vma=False,
    )
```

time: 89.3 us -> 77.6 us (0.87)
  Pallas kernels: 81.3 us -> 73.6 us
  local copies, waits for them, and re-layouts: 7.1 us -> 3.24 us
    pallas_call x1, Pallas kernels: 81.3 us -> 73.6 us  [per_device(): pl.pallas_call(lambda *refs: block_kernel(math.sqrt(cell_count), *refs),...]
    unnamed x11 -> x4, local copies, waits for them, and re-layouts: 6.41 us -> 3.24 us
where the time goes in v3:
time: 77.6 us; the launch traced here: 77.4 us
  Pallas kernels  73.6 us (95%)
  local copies, waits for them, and re-layouts  3.24 us (4%)
    pallas_call x1, Pallas kernels, per_device(): pl.pallas_call(lambda *refs: block_kernel(math.sqrt(cell_count), *refs),...  73.6 us
    unnamed x4, local copies, waits for them, and re-layouts  3.24 us

profile of v3, /device:TPU:1, one launch (start us, length us, event | category | flops | bytes accessed | tf_op | source)
XLA Modules:
  0.0 77.4 jit_solution(3256876837308702260)
XLA Ops:
  0.6 73.6 %shard_map.77 = (bf16[80,16,384]{2,1,0:T(8,128)(2,1)}, bf16[1152,384]{1,0:T(8,128)(2,1)}) custom-call(bf16[80,16,384]{2,1,0:T(8,128)(2,1)} %refs_0_.1, bf16[5,17,3,320]{3,2,1,0:T(4,128)(2,1)} %bitcast.1, s32[320]{0:T(512)} %refs_2_.1, bf16[1152,384]{1,0:T(8,128)(2,1)} %refs_3_.1, f32[384]{0:T(512)} %refs_4_.1, bf16[80,16,384]{2,1,0:T(8,128)(2,1)} %refs_5_.1), custom_call_target="tpu_custom_call" | custom-call | tf_op jit(solution)/shard_map/pallas_call | solution.py:470
  74.2 0.0 copy-start
  74.2 2.3 %copy.10 = bf16[80,16,384]{2,1,0:T(8,128)(2,1)} copy(bf16[80,16,384]{2,1,0:T(8,128)(2,1)} %get-tuple-element.4) | data formatting | bytes 1966080
  76.5 0.0 copy-done
  76.5 0.9 %copy.11 = bf16[1152,384]{1,0:T(8,128)(2,1)} copy(bf16[1152,384]{1,0:T(8,128)(2,1)S(1)} %copy-done) | data formatting | bytes 1769472
Async XLA Ops:
  74.2 2.3 %copy-start = (bf16[1152,384]{1,0:T(8,128)(2,1)S(1)}, bf16[1152,384]{1,0:T(8,128)(2,1)}, u32[]{:S(2)}) copy-start(bf16[1152,384]{1,0:T(8,128)(2,1)} %get-tuple-element.5) | copy-start | bytes 2654212

commit v4 on v3

--- a/solution.py
+++ b/solution.py
@@ -222,7 +222,7 @@
         self.own, self.west_in, self.east_in = own, west_in, east_in
         self.west_out, self.east_out, self.send, self.recv = west_out, east_out, send, recv
         self.peers, self.rows, self.cuts, self.used = halo_peers(), own.shape[0] - 4, cuts, 0
-        self.pairs, self.parts, self.top, self.bottom = self.rows // 2, [], [], []
+        self.pairs, self.parts, self.top, self.bottom, self.sent = self.rows // 2, [], [], [], []
 
     def copy(self, src, dst, peer):
         index = self.used
@@ -231,7 +231,17 @@
             src_ref=src, dst_ref=dst, send_sem=self.send.at[index], recv_sem=self.recv.at[index],
             device_id=self.peers[peer], device_id_type=MESH)
         copy.start()
+        self.sent.append(copy)
         return copy
+
+    def left(self, part):
+        for copy in self.parts[part]:
+            copy.wait_send()
+            self.sent = [other for other in self.sent if other is not copy]
+
+    def drain(self):
+        for copy in self.sent:
+            copy.wait_send()
 
     def pack(self, first, values):
         pairs, channels = values.shape[0] // 2, values.shape[-1]
@@ -264,7 +274,7 @@
 
     def wait(self, copies):
         for copy in copies:
-            copy.wait()
+            copy.wait_recv()
 
     def window(self, first):
         channels = self.own.shape[-1]
@@ -376,20 +386,31 @@
     work.clear()
     await_greetings(len(peers))
     halo.send_north()
-    for part in range(parts):
-        halo.send_part(part)
     halo.send_south()
+    halo.send_part(0)
+    halo.send_part(1)
 
     first = pl.multiple_of(lax.axis_index("lat") * rows, 8)
     loads[1].wait()
     lay_taps(filter_basis, half_widths, stage, taps)
     lay_band(taps, base, moved, band, first, rows, total_rows, False)
+    for part in (0, 1):
+        halo.left(part)
+        halo.send_part(part + 2)
     loads[2].wait()
     loads[3].wait()
     halo.wait(halo.top)
     cells = part_rows * width
     for part in range(parts):
         halo.wait(halo.parts[part])
+        if part == 1:
+            halo.left(2)
+            halo.send_part(4)
+        if part == parts - 1:
+            halo.left(4)
+            for packed in range(part):
+                g_halo.send_part(packed)
+            g_halo.send_north()
         if part == parts - 1:
             halo.wait(halo.bottom)
         apply_blocks(band, halo, flat, part, channels, blocks)
@@ -402,10 +423,8 @@
         grad = grad.astype(jnp.bfloat16)
         g_own[2 + at : 2 + at + part_rows] = grad.reshape(part_rows, width, channels)
         g_halo.pack(at // 2, grad_rows)
-        g_halo.send_part(part)
-        if part == 0:
-            g_halo.send_north()
         if part == parts - 1:
+            g_halo.send_part(part)
             g_halo.send_south()
         outer = lax.dot_general(here, grad, (((0,), (0,)), ((), ())), preferred_element_type=jnp.float32)
         if part == 0:
@@ -419,7 +438,8 @@
     work.core_to_x()
     lay_band(taps, base, moved, g_band, first, rows, total_rows, True)
     work.x_to_y()
-    steps = {1: work.y_to_z, 3: work.z_to_gather, 4: work.gather_y}
+    work.y_to_z()
+    steps = {3: work.z_to_gather, 4: work.gather_y}
     stores = []
     g_halo.wait(g_halo.top)
     g_halo.wait(g_halo.parts[0])
@@ -446,6 +466,8 @@
     work.finish(mixing_out)
     for store in stores:
         store.wait()
+    halo.drain()
+    g_halo.drain()
 
 
 def halo_buffers(rows, channels, parts):

time: 77.6 us -> 77 us (level)
  no operation moved by 1% of the time
where the time goes in v4:
time: 77 us; the launch traced here: 76.8 us
  Pallas kernels  73 us (95%)
  local copies, waits for them, and re-layouts  3.24 us (4%)
    pallas_call x1, Pallas kernels, per_device(): pl.pallas_call(lambda *refs: block_kernel(math.sqrt(cell_count), *refs),...  73 us
    unnamed x4, local copies, waits for them, and re-layouts  3.24 us

profile of v4, /device:TPU:1, one launch (start us, length us, event | category | flops | bytes accessed | tf_op | source)
XLA Modules:
  0.0 76.8 jit_solution(13294588526400596397)
XLA Ops:
  0.6 73.0 %shard_map.77 = (bf16[80,16,384]{2,1,0:T(8,128)(2,1)}, bf16[1152,384]{1,0:T(8,128)(2,1)}) custom-call(bf16[80,16,384]{2,1,0:T(8,128)(2,1)} %refs_0_.1, bf16[5,17,3,320]{3,2,1,0:T(4,128)(2,1)} %bitcast.1, s32[320]{0:T(512)} %refs_2_.1, bf16[1152,384]{1,0:T(8,128)(2,1)} %refs_3_.1, f32[384]{0:T(512)} %refs_4_.1, bf16[80,16,384]{2,1,0:T(8,128)(2,1)} %refs_5_.1), custom_call_target="tpu_custom_call" | custom-call | tf_op jit(solution)/shard_map/pallas_call | solution.py:492
  73.6 0.0 copy-start
  73.6 2.3 %copy.10 = bf16[80,16,384]{2,1,0:T(8,128)(2,1)} copy(bf16[80,16,384]{2,1,0:T(8,128)(2,1)} %get-tuple-element.4) | data formatting | bytes 1966080
  75.9 0.0 copy-done
  75.9 0.9 %copy.11 = bf16[1152,384]{1,0:T(8,128)(2,1)} copy(bf16[1152,384]{1,0:T(8,128)(2,1)S(1)} %copy-done) | data formatting | bytes 1769472
Async XLA Ops:
  73.6 2.3 %copy-start = (bf16[1152,384]{1,0:T(8,128)(2,1)S(1)}, bf16[1152,384]{1,0:T(8,128)(2,1)}, u32[]{:S(2)}) copy-start(bf16[1152,384]{1,0:T(8,128)(2,1)} %get-tuple-element.5) | copy-start | bytes 2654212

commit v5 on v4

--- a/solution.py
+++ b/solution.py
@@ -407,11 +407,6 @@
             halo.left(2)
             halo.send_part(4)
         if part == parts - 1:
-            halo.left(4)
-            for packed in range(part):
-                g_halo.send_part(packed)
-            g_halo.send_north()
-        if part == parts - 1:
             halo.wait(halo.bottom)
         apply_blocks(band, halo, flat, part, channels, blocks)
         here = flat[part * cells : (part + 1) * cells]
@@ -423,8 +418,10 @@
         grad = grad.astype(jnp.bfloat16)
         g_own[2 + at : 2 + at + part_rows] = grad.reshape(part_rows, width, channels)
         g_halo.pack(at // 2, grad_rows)
+        g_halo.send_part(part)
+        if part == 0:
+            g_halo.send_north()
         if part == parts - 1:
-            g_halo.send_part(part)
             g_halo.send_south()
         outer = lax.dot_general(here, grad, (((0,), (0,)), ((), ())), preferred_element_type=jnp.float32)
         if part == 0:
@@ -439,7 +436,7 @@
     lay_band(taps, base, moved, g_band, first, rows, total_rows, True)
     work.x_to_y()
     work.y_to_z()
-    steps = {3: work.z_to_gather, 4: work.gather_y}
+    steps = {2: work.z_to_gather, 3: work.gather_y}
     stores = []
     g_halo.wait(g_halo.top)
     g_halo.wait(g_halo.parts[0])

time: 77 us -> 72.8 us (0.945)
  Pallas kernels: 73 us -> 68.7 us
    pallas_call x1, Pallas kernels: 73 us -> 68.7 us  [per_device(): pl.pallas_call(lambda *refs: block_kernel(math.sqrt(cell_count), *refs),...]
where the time goes in v5:
time: 72.8 us; the launch traced here: 72.6 us
  Pallas kernels  68.7 us (94%)
  local copies, waits for them, and re-layouts  3.24 us (4%)
    pallas_call x1, Pallas kernels, per_device(): pl.pallas_call(lambda *refs: block_kernel(math.sqrt(cell_count), *refs),...  68.7 us
    unnamed x4, local copies, waits for them, and re-layouts  3.24 us

profile of v5, /device:TPU:1, one launch (start us, length us, event | category | flops | bytes accessed | tf_op | source)
XLA Modules:
  0.0 72.6 jit_solution(7081820860751817724)
XLA Ops:
  0.6 68.7 %shard_map.77 = (bf16[80,16,384]{2,1,0:T(8,128)(2,1)}, bf16[1152,384]{1,0:T(8,128)(2,1)}) custom-call(bf16[80,16,384]{2,1,0:T(8,128)(2,1)} %refs_0_.1, bf16[5,17,3,320]{3,2,1,0:T(4,128)(2,1)} %bitcast.1, s32[320]{0:T(512)} %refs_2_.1, bf16[1152,384]{1,0:T(8,128)(2,1)} %refs_3_.1, f32[384]{0:T(512)} %refs_4_.1, bf16[80,16,384]{2,1,0:T(8,128)(2,1)} %refs_5_.1), custom_call_target="tpu_custom_call" | custom-call | tf_op jit(solution)/shard_map/pallas_call | solution.py:489
  69.3 0.0 copy-start
  69.3 2.3 %copy.10 = bf16[80,16,384]{2,1,0:T(8,128)(2,1)} copy(bf16[80,16,384]{2,1,0:T(8,128)(2,1)} %get-tuple-element.4) | data formatting | bytes 1966080
  71.7 0.0 copy-done
  71.7 0.9 %copy.11 = bf16[1152,384]{1,0:T(8,128)(2,1)} copy(bf16[1152,384]{1,0:T(8,128)(2,1)S(1)} %copy-done) | data formatting | bytes 1769472
Async XLA Ops:
  69.3 2.3 %copy-start = (bf16[1152,384]{1,0:T(8,128)(2,1)S(1)}, bf16[1152,384]{1,0:T(8,128)(2,1)}, u32[]{:S(2)}) copy-start(bf16[1152,384]{1,0:T(8,128)(2,1)} %get-tuple-element.5) | copy-start | bytes 2654212

commit v6 on v5

--- a/solution.py
+++ b/solution.py
@@ -77,15 +77,19 @@
         self.rows, self.lanes, self.tiles, self.scale = rows, channels // 128, tile_count(rows, channels), scale
         self.x, self.z, self.y, self.core = position()
         self.used, self.sent = 0, []
-
-    def copy(self, src, dst, peer):
+        self.mine = self.has(self.y)
+
+    def has(self, y):
+        return y < SIZE_Y - 1
+
+    def copy(self, when, src, dst, peer):
         index = self.used
         self.used += 1
         copy = pltpu.make_async_remote_copy(
             src_ref=src, dst_ref=dst, send_sem=self.send.at[index], recv_sem=self.recv.at[index],
             device_id=peer, device_id_type=MESH)
-        copy.start()
-        self.sent.append(copy)
+        pl.when(when)(copy.start)
+        self.sent.append((when, copy))
         return copy
 
     def other_core(self):
@@ -119,18 +123,22 @@
         self.from_core = {}
         for d in Y_ORDER:
             y = lax.rem(self.y + d, SIZE_Y)
-            self.from_core[d] = self.copy(self.local.at[1 - self.core, y], self.half.at[y], self.other_core())
+            self.from_core[d] = self.copy(self.has(y), self.local.at[1 - self.core, y], self.half.at[y], self.other_core())
 
     def core_to_x(self):
         self.from_x = {}
         for d in Y_ORDER:
             y = lax.rem(self.y + d, SIZE_Y)
-            self.from_core[d].wait_recv()
-            total = self.half[y] + self.local[self.core, y]
-            self.half[y] = total
-            self.x_out[y] = total.astype(jnp.bfloat16)
+
+            @pl.when(self.has(y))
+            def _(d=d, y=y):
+                self.from_core[d].wait_recv()
+                total = self.half[y] + self.local[self.core, y]
+                self.half[y] = total
+                self.x_out[y] = total.astype(jnp.bfloat16)
+
             self.from_x[d] = [
-                self.copy(self.x_out.at[y, lax.rem(self.x + e, SIZE_X)], self.x_in.at[e - 1, y], self.other_x(e))
+                self.copy(self.has(y), self.x_out.at[y, lax.rem(self.x + e, SIZE_X)], self.x_in.at[e - 1, y], self.other_x(e))
                 for e in (2, 1, 3)
             ]
 
@@ -138,70 +146,81 @@
         self.from_y = []
         for d in Y_ORDER:
             y = lax.rem(self.y + d, SIZE_Y)
-            total = self.half[y, self.x]
-            for copy in self.from_x[d]:
+
+            @pl.when(self.has(y))
+            def _(d=d, y=y):
+                total = self.half[y, self.x]
+                for copy in self.from_x[d]:
+                    copy.wait_recv()
+                for e in range(SIZE_X - 1):
+                    total = total + self.x_in[e, y].astype(jnp.float32)
+                if d:
+                    self.y_out[d - 1] = total.astype(jnp.bfloat16)
+                else:
+                    self.half[y, self.x] = total
+
+            if d:
+                self.from_y.append(self.copy(self.has(y), self.y_out.at[d - 1], self.y_in.at[d - 1], self.other_y(d)))
+
+    def y_to_z(self):
+        @pl.when(self.mine)
+        def _():
+            total = self.half[self.y, self.x]
+            for copy in self.from_y:
                 copy.wait_recv()
-            for e in range(SIZE_X - 1):
-                total = total + self.x_in[e, y].astype(jnp.float32)
-            if d:
-                self.y_out[d - 1] = total.astype(jnp.bfloat16)
-                self.from_y.append(self.copy(self.y_out.at[d - 1], self.y_in.at[d - 1], self.other_y(d)))
-            else:
-                self.half[y, self.x] = total
-
-    def y_to_z(self):
-        total = self.half[self.y, self.x]
-        for copy in self.from_y:
-            copy.wait_recv()
-        for d in range(SIZE_Y - 1):
-            total = total + self.y_in[d].astype(jnp.float32)
-        self.z_all[self.z] = total.astype(jnp.bfloat16)
+            for d in range(SIZE_Y - 1):
+                total = total + self.y_in[d].astype(jnp.float32)
+            self.z_all[self.z] = total.astype(jnp.bfloat16)
+
         piece = self.z_all.at[self.z]
-        self.from_z = [self.copy(piece, piece, self.other_z(d)) for d in (4, 3, 5, 2, 6, 1, 7)]
+        self.from_z = [self.copy(self.mine, piece, piece, self.other_z(d)) for d in (4, 3, 5, 2, 6, 1, 7)]
 
     def spread_x(self, d):
         y = lax.rem(self.y + SIZE_Y - d, SIZE_Y)
         piece = self.done.at[self.core, self.x, y]
         for e in (2, 1, 3):
-            self.gathered[e].append(self.copy(piece, piece, self.other_x(e)))
+            self.gathered[e].append(self.copy(self.has(y), piece, piece, self.other_x(e)))
 
     def z_to_gather(self):
-        for copy in self.from_z:
-            copy.wait_recv()
-        total = self.z_all[0].astype(jnp.float32)
-        for other in range(1, SIZE_Z):
-            total = total + self.z_all[other].astype(jnp.float32)
-        self.done[self.core, self.x, self.y] = (total / self.scale).astype(jnp.bfloat16)
+        @pl.when(self.mine)
+        def _():
+            for copy in self.from_z:
+                copy.wait_recv()
+            total = self.z_all[0].astype(jnp.float32)
+            for other in range(1, SIZE_Z):
+                total = total + self.z_all[other].astype(jnp.float32)
+            self.done[self.core, self.x, self.y] = (total / self.scale).astype(jnp.bfloat16)
+
         piece = self.done.at[self.core, self.x, self.y]
-        self.y_gathered = {d: self.copy(piece, piece, self.other_y(d)) for d in (4, 3, 5, 2, 6, 1, 7)}
+        self.y_gathered = {d: self.copy(self.mine, piece, piece, self.other_y(d)) for d in (4, 3, 5, 2, 6, 1, 7)}
         self.gathered = {e: [] for e in range(1, SIZE_X)}
         self.spread_x(0)
 
     def gather_y(self):
         for d in GATHER_ORDER[1:]:
-            self.y_gathered[d].wait_recv()
+            pl.when(self.has(lax.rem(self.y + SIZE_Y - d, SIZE_Y)))(self.y_gathered[d].wait_recv)
             self.spread_x(d)
         self.spread_core(0)
 
     def spread_core(self, e):
-        part = self.done.at[self.core, lax.rem(self.x + SIZE_X - e, SIZE_X)]
-        self.copy(part, part, self.other_core())
+        part = self.done.at[self.core, lax.rem(self.x + SIZE_X - e, SIZE_X), 0 : SIZE_Y - 1]
+        self.copy(self.core >= 0, part, part, self.other_core())
 
     def gather_x(self):
         for e in (1, 3, 2):
-            for copy in self.gathered[e]:
-                copy.wait_recv()
+            for d, copy in zip(GATHER_ORDER, self.gathered[e]):
+                pl.when(self.has(lax.rem(self.y + SIZE_Y - d, SIZE_Y)))(copy.wait_recv)
             self.spread_core(e)
 
     def finish(self, out):
-        for copy in self.sent[-SIZE_X:]:
+        for _, copy in self.sent[-SIZE_X:]:
             copy.wait_recv()
         for core in range(2):
             for part in range(SIZE_X):
                 for y, slot, rows, lanes in self.places(core, part):
                     out[rows, lanes] = self.done[core, part, y, slot]
-        for copy in self.sent:
-            copy.wait_send()
+        for when, copy in self.sent:
+            pl.when(when)(copy.wait_send)
 
 
 def halo_peers():

time: 72.8 us -> 72.6 us (level)
  no operation moved by 1% of the time
where the time goes in v6:
time: 72.6 us; the launch traced here: 72.5 us
  Pallas kernels  68.6 us (94%)
  local copies, waits for them, and re-layouts  3.24 us (4%)
    pallas_call x1, Pallas kernels, per_device(): pl.pallas_call(lambda *refs: block_kernel(math.sqrt(cell_count), *refs),...  68.6 us
    unnamed x4, local copies, waits for them, and re-layouts  3.24 us

profile of v6, /device:TPU:1, one launch (start us, length us, event | category | flops | bytes accessed | tf_op | source)
XLA Modules:
  0.0 72.5 jit_solution(17106511666659857617)
XLA Ops:
  0.6 68.6 %shard_map.77 = (bf16[80,16,384]{2,1,0:T(8,128)(2,1)}, bf16[1152,384]{1,0:T(8,128)(2,1)}) custom-call(bf16[80,16,384]{2,1,0:T(8,128)(2,1)} %refs_0_.1, bf16[5,17,3,320]{3,2,1,0:T(4,128)(2,1)} %bitcast.1, s32[320]{0:T(512)} %refs_2_.1, bf16[1152,384]{1,0:T(8,128)(2,1)} %refs_3_.1, f32[384]{0:T(512)} %refs_4_.1, bf16[80,16,384]{2,1,0:T(8,128)(2,1)} %refs_5_.1), custom_call_target="tpu_custom_call" | custom-call | tf_op jit(solution)/shard_map/pallas_call | solution.py:508
  69.2 0.0 copy-start
  69.2 2.3 %copy.10 = bf16[80,16,384]{2,1,0:T(8,128)(2,1)} copy(bf16[80,16,384]{2,1,0:T(8,128)(2,1)} %get-tuple-element.4) | data formatting | bytes 1966080
  71.5 0.0 copy-done
  71.5 0.9 %copy.11 = bf16[1152,384]{1,0:T(8,128)(2,1)} copy(bf16[1152,384]{1,0:T(8,128)(2,1)S(1)} %copy-done) | data formatting | bytes 1769472
Async XLA Ops:
  69.2 2.3 %copy-start = (bf16[1152,384]{1,0:T(8,128)(2,1)S(1)}, bf16[1152,384]{1,0:T(8,128)(2,1)}, u32[]{:S(2)}) copy-start(bf16[1152,384]{1,0:T(8,128)(2,1)} %get-tuple-element.5) | copy-start | bytes 2654212

commit v7 on v6

--- a/solution.py
+++ b/solution.py
@@ -390,8 +390,7 @@
         pltpu.make_async_copy(mixing_hbm, mixing, load_sem.at[1]),
         pltpu.make_async_copy(cotangent_hbm, cotangent, load_sem.at[2]),
     ]
-    for load in loads:
-        load.start()
+    loads[0].start()
     peers = list(halo_peers().values()) + sum_peers()
     greet(peers)
     work = SumOverAll(mixing.shape[0] // (2 * SIZE_X), channels, sum_refs, scale)
@@ -399,6 +398,8 @@
     halo = Halo(own, west_in, east_in, west_out, east_out, send, recv, cuts)
     g_halo = Halo(g_own, g_west_in, g_east_in, g_west_out, g_east_out, g_send, g_recv, [pairs * part for part in range(parts + 1)])
     loads[0].wait()
+    for load in loads[1:]:
+        load.start()
     for part in range(parts):
         lo, hi = cuts[part], cuts[part + 1]
         halo.pack(lo, own[2 + 2 * lo : 2 + 2 * hi].astype(jnp.float32))
@@ -422,8 +423,7 @@
     cells = part_rows * width
     for part in range(parts):
         halo.wait(halo.parts[part])
-        if part == 1:
-            halo.left(2)
+        if part == 0:
             halo.send_part(4)
         if part == parts - 1:
             halo.wait(halo.bottom)

time: 72.6 us -> 72.7 us (level)
  no operation moved by 1% of the time
where the time goes in v7:
time: 72.7 us; the launch traced here: 72.5 us
  Pallas kernels  68.6 us (94%)
  local copies, waits for them, and re-layouts  3.24 us (4%)
    pallas_call x1, Pallas kernels, per_device(): pl.pallas_call(lambda *refs: block_kernel(math.sqrt(cell_count), *refs),...  68.6 us
    unnamed x4, local copies, waits for them, and re-layouts  3.24 us

profile of v7, /device:TPU:1, one launch (start us, length us, event | category | flops | bytes accessed | tf_op | source)
XLA Modules:
  0.0 72.5 jit_solution(18377214678804787052)
XLA Ops:
  0.6 68.6 %shard_map.77 = (bf16[80,16,384]{2,1,0:T(8,128)(2,1)}, bf16[1152,384]{1,0:T(8,128)(2,1)}) custom-call(bf16[80,16,384]{2,1,0:T(8,128)(2,1)} %refs_0_.1, bf16[5,17,3,320]{3,2,1,0:T(4,128)(2,1)} %bitcast.1, s32[320]{0:T(512)} %refs_2_.1, bf16[1152,384]{1,0:T(8,128)(2,1)} %refs_3_.1, f32[384]{0:T(512)} %refs_4_.1, bf16[80,16,384]{2,1,0:T(8,128)(2,1)} %refs_5_.1), custom_call_target="tpu_custom_call" | custom-call | tf_op jit(solution)/shard_map/pallas_call | solution.py:508
  69.3 0.0 copy-start
  69.3 2.3 %copy.10 = bf16[80,16,384]{2,1,0:T(8,128)(2,1)} copy(bf16[80,16,384]{2,1,0:T(8,128)(2,1)} %get-tuple-element.4) | data formatting | bytes 1966080
  71.6 0.0 copy-done
  71.6 0.9 %copy.11 = bf16[1152,384]{1,0:T(8,128)(2,1)} copy(bf16[1152,384]{1,0:T(8,128)(2,1)S(1)} %copy-done) | data formatting | bytes 1769472
Async XLA Ops:
  69.3 2.3 %copy-start = (bf16[1152,384]{1,0:T(8,128)(2,1)S(1)}, bf16[1152,384]{1,0:T(8,128)(2,1)}, u32[]{:S(2)}) copy-start(bf16[1152,384]{1,0:T(8,128)(2,1)} %get-tuple-element.5) | copy-start | bytes 2654212
